TPU v7x, 128 devices: a whole 4x4x4 slice. The times are simulated.
128 devices in a mesh: slab: 8 (over x_hi, z), col: 16 (over x_lo, y, core).
Axes of the slice: x: 4 (x_hi: 2, x_lo: 2; x = x_hi * 2 + x_lo), y: 4, z: 4, core: 2. Of those that a mesh axis runs over, the one named last changes fastest.
Arguments:
- volume: bfloat16 [64, 2097152], P('slab', 'col'), may hold values from -6 to 6
- consensus: bfloat16 [64, 2097152], P('slab', 'col'), may hold values from -6 to 6
- templates: bfloat16 [128, 1024, 128], P('col'), may hold values from -0.015625 to 0.015625
- pattern: int32 [16, 256, 8, 8], P('col'), may hold values from 0 to 1023
- probe_wave: float32 [2, 64, 64], replicated, may hold values from -6 to 6
- measured: float32 [256, 128, 64, 64], P(('slab', 'col')), may hold values from 0.1 to 4
- scan_counts: int32 [256], replicated, may hold values from 1 to 128, as said below
- scan_positions: int32 [256, 128], replicated, may hold values from 0 to 960
Outputs:
- updated: float32 [64, 2097152], P('slab', 'col')
Inputs may be any that keep to these rules, and one draw needn't show every extreme that they name: scan_counts[a] positions are used at angle a; 128 is reached by some angle in every draw. `scan_positions`: only the first scan_counts[a] entries of row a are used. `pattern`: entry t * 8 + k names template k of the column group applied to its volume tile t.
All inputs are finite; a program needn't handle non-finite values.
Results may differ from a plain program's by a relative error of at most 0.0044.
Values may be sent and summed in bfloat16 or wider, within the bound.
A program may use at most 128 MiB of HBM per device.

v0:
```python
import math

import jax
import jax.numpy as jnp
from jax import lax
from jax.sharding import PartitionSpec as P

step_size = 0.1
penalty = 1.0


def dft_tables(length):
    grid_index = jnp.arange(length, dtype=jnp.int32)
    product = grid_index[:, None] * grid_index[None, :] % length
    radians = 2.0 * math.pi / length * product.astype(jnp.float32)
    norm_scale = 1.0 / math.sqrt(length)
    cosine_part = jnp.cos(radians) * norm_scale
    sine_part = jnp.sin(radians) * norm_scale
    forward = jnp.concatenate(
        [
            jnp.concatenate([cosine_part, -sine_part], 1),
            jnp.concatenate([sine_part, cosine_part], 1),
        ],
        0,
    )
    inverse = jnp.concatenate(
        [
            jnp.concatenate([cosine_part, sine_part], 1),
            jnp.concatenate([-sine_part, cosine_part], 1),
        ],
        0,
    )
    return (forward, inverse)


def along_last(real_part, imag_part, dft_table):
    stacked = jnp.concatenate([real_part, imag_part], -1)
    result = jnp.matmul(stacked, dft_table, precision=lax.Precision.HIGHEST)
    half_width = real_part.shape[-1]
    return (result[..., :half_width], result[..., half_width:])


def transform_both(real_part, imag_part, dft_table):
    real_part, imag_part = along_last(real_part, imag_part, dft_table)
    real_part, imag_part = along_last(
        jnp.swapaxes(real_part, -1, -2), jnp.swapaxes(imag_part, -1, -2), dft_table
    )
    return (jnp.swapaxes(real_part, -1, -2), jnp.swapaxes(imag_part, -1, -2))


def angle_gradient(
    phase_image, measured_angle, live_count, positions, probe_wave, forward, inverse, block_size
):
    slice_count, detector_width = phase_image.shape
    patch_size = probe_wave.shape[-1]
    offsets = jnp.arange(patch_size, dtype=jnp.int32)
    block_lanes = jnp.arange(block_size, dtype=jnp.int32)
    detector_index = jnp.arange(detector_width, dtype=jnp.int32)

    def block_step(block_number, gradient):
        block_start = block_number * block_size
        starts = lax.dynamic_slice_in_dim(positions, block_start, block_size)
        columns = (starts[:, None] + offsets[None, :]).reshape(-1)
        patch_phase = (
            jnp.take(phase_image, columns, axis=1)
            .reshape(slice_count, block_size, patch_size)
            .transpose(1, 0, 2)
        )
        cosine_part = jnp.cos(patch_phase)
        sine_part = jnp.sin(patch_phase)
        wave_real = probe_wave[0] * cosine_part - probe_wave[1] * sine_part
        wave_imag = probe_wave[0] * sine_part + probe_wave[1] * cosine_part
        spec_real, spec_imag = transform_both(wave_real, wave_imag, forward)
        observed = lax.dynamic_slice_in_dim(measured_angle, block_start, block_size)
        residual = spec_real * spec_real + spec_imag * spec_imag - observed
        back_real, back_imag = transform_both(residual * spec_real, residual * spec_imag, inverse)
        patch_grad = 2.0 * (wave_real * back_imag - wave_imag * back_real)
        is_live = block_start + block_lanes < live_count
        patch_grad = jnp.where(is_live[:, None, None], patch_grad, 0.0)
        flat_grad = patch_grad.transpose(1, 0, 2).reshape(slice_count, block_size * patch_size)
        placement = (columns[:, None] == detector_index[None, :]).astype(jnp.float32)
        return gradient + jnp.dot(flat_grad, placement, precision=lax.Precision.HIGHEST)

    blocks = (live_count + block_size - 1) // block_size
    return lax.fori_loop(
        0, blocks, block_step, jnp.zeros((slice_count, detector_width), jnp.float32)
    )


def ptycho_step(images, measured, angle_ids, probe_wave, scan_counts, scan_positions):
    forward, inverse = dft_tables(probe_wave.shape[-1])
    block_size = math.gcd(measured.shape[1], 16)
    counts = scan_counts[angle_ids]
    positions = scan_positions[angle_ids]
    slot_grads = []
    for number in range(images.shape[1]):
        slot_grads.append(
            angle_gradient(
                images[:, number, :],
                measured[number],
                counts[number],
                positions[number],
                probe_wave,
                forward,
                inverse,
                block_size,
            )
        )
    return jnp.stack(slot_grads, 1).astype(jnp.bfloat16)


def on_device(
    volume, consensus, templates, pattern, probe_wave, measured, scan_counts, scan_positions
):
    slab_rows, cell_count = volume.shape
    group_templates, tile_cells, tile_width = templates.shape
    slab_count = lax.axis_size("slab")
    column_count = lax.axis_size("col")
    layout = pattern[0]
    angle_count, tile_rows, spread = layout.shape
    detector_width = tile_rows * tile_width
    slice_count = slab_rows * slab_count
    per_owner = angle_count // (slab_count * column_count)
    tile_count = cell_count // tile_cells
    segments = tile_count * group_templates
    segment_index = jnp.arange(segments, dtype=jnp.int32)
    layout_rows = layout.reshape(angle_count * tile_rows, spread)
    count_matrix = jnp.zeros((angle_count * tile_rows, segments), jnp.bfloat16)
    for member in range(spread):
        count_matrix = count_matrix + (
            layout_rows[:, member, None] == segment_index[None, :]
        ).astype(jnp.bfloat16)
    volume_tiles = volume.reshape(slab_rows, tile_count, tile_cells)
    tile_table = jnp.einsum(
        "ztv,kvd->ztkd", volume_tiles, templates, preferred_element_type=jnp.float32
    )
    tile_table = tile_table.astype(jnp.bfloat16).reshape(slab_rows, segments, tile_width)
    partial_value = jnp.einsum(
        "rs,zsd->zrd", count_matrix, tile_table, preferred_element_type=jnp.float32
    )
    partial_value = partial_value.reshape(
        slab_rows, slab_count, column_count, per_owner * detector_width
    )
    summed = lax.psum(partial_value, "col")
    regrouped = lax.all_to_all(summed, "slab", split_axis=1, concat_axis=0, tiled=True)
    owned = lax.dynamic_slice_in_dim(regrouped, lax.axis_index("col"), 1, 2)
    images = owned.reshape(slice_count, per_owner, detector_width)
    slab_index = lax.axis_index("slab")
    column_index = lax.axis_index("col")
    owner_index = slab_index * column_count + column_index
    slot_index = jnp.arange(per_owner, dtype=jnp.int32)
    local_ids = owner_index * per_owner + slot_index
    gradients = ptycho_step(images, measured, local_ids, probe_wave, scan_counts, scan_positions)
    outgoing = gradients.reshape(slice_count, per_owner, tile_rows, tile_width).transpose(
        1, 2, 0, 3
    )
    outgoing = outgoing.reshape(1, 1, per_owner, tile_rows, slice_count, tile_width)
    incoming = lax.all_to_all(outgoing, "slab", split_axis=4, concat_axis=0, tiled=True)
    count_grid = count_matrix.reshape(slab_count, column_count, per_owner * tile_rows, segments)
    chosen = count_grid.reshape(-1, segments)
    rows_data = lax.all_gather(incoming, "col", axis=1, tiled=True).reshape(
        -1, slab_rows * tile_width
    )
    gathered = lax.dot_general(
        chosen, rows_data, (((0,), (0,)), ((), ())), preferred_element_type=jnp.float32
    )
    rounded = gathered.astype(jnp.bfloat16).reshape(
        tile_count, group_templates, slab_rows, tile_width
    )
    backproj = jnp.einsum(
        "tkzd,kvd->ztv", rounded, templates, preferred_element_type=jnp.float32
    ).reshape(slab_rows, cell_count)
    volume_f32 = volume.astype(jnp.float32)
    return volume_f32 - step_size * (
        backproj + penalty * (volume_f32 - consensus.astype(jnp.float32))
    )


def solution(mesh):
    return jax.shard_map(
        on_device,
        mesh=mesh,
        in_specs=(
            P("slab", "col"),
            P("slab", "col"),
            P("col", None, None),
            P("col", None, None, None),
            P(),
            P(("slab", "col"), None, None, None),
            P(),
            P(),
        ),
        out_specs=P("slab", "col"),
        check_vma=False,
    )
```

profile of v0, /device:TPU:1, one launch (start us, length us, event | category | flops | bytes accessed | tf_op | source)
XLA Modules:
  0.0 757.3 jit_solution(3661397259965905692)
XLA Ops:
  8.5 5.2 fusion.116
  13.8 14.5 %convolution_bitcast_fusion = f32[8,2048,128]{1,2,0:T(8,128)} fusion(bf16[8,128,8,128]{3,1,2,0:T(8,128)(2,1)S(1)} %fusion.116, s32[2048]{0:T(1024)S(1)} %bitcast.267, s32[2048]{0:T(1024)S(1)} %bitcast.269, s32[2048]{0:T(1024)S(1)} %bitcast.271, s32[2048]{0:T(1024)S(1)} %bitcast.273, s32[2048]{0:T(1024)S(1)} %bitcast.275, s32[2048]{0:T(1024)S(1)} %bitcast.277, ...), kind=kOutput, calls=%fused_computation.144 | convolution fusion | flops 4362076160 | bytes 10551296 | tf_op jit(solution)/shard_map/rs,zsd->zrd/dot_general | solution.py:138
  28.4 9.1 %copy.194 = f32[8,2048,128]{2,1,0:T(8,128)} copy(f32[8,2048,128]{1,2,0:T(8,128)} %convolution_bitcast_fusion) | data formatting | bytes 16777216 | tf_op jit(solution)/shard_map/rs,zsd->zrd/transpose | solution.py:138
  37.5 9.3 %reshape.120 = f32[8,8,16,2048]{3,2,1,0:T(8,128)} reshape(f32[8,2048,128]{2,1,0:T(8,128)} %copy.194) | data formatting | bytes 16777216 | tf_op jit(solution)/shard_map/reshape | solution.py:141
  46.9 144.6 %all-reduce.2.cloned.1.call-done = f32[8,8,16,2048]{3,2,1,0:T(8,128)} async-done(((f32[8,8,16,2048]{3,2,1,0:T(8,128)}), f32[8,8,16,2048]{3,2,1,0:T(8,128)}) %all-reduce.2.cloned.1.call-update) | async-done | bytes 8388624 | tf_op jit(solution)/shard_map/psum | solution.py:144
  191.5 7.8 %copy.195 = f32[8,8,16,2048]{3,2,0,1:T(8,128)} copy(f32[8,8,16,2048]{3,2,1,0:T(8,128)} %all-reduce.2.cloned.1.call-done) | data formatting | bytes 16777216 | tf_op jit(solution)/shard_map/psum | solution.py:144
  199.3 6.4 all-to-all-start
  209.7 4.8 fusion.135
  214.5 5.6 copy.220
  220.1 5.7 copy.221
  226.7 72.6 %all-to-all-done = f32[8,8,16,2048]{3,2,0,1:T(8,128)} async-done(((f32[8,8,16,2048]{3,2,0,1:T(8,128)}), f32[8,8,16,2048]{3,2,0,1:T(8,128)}, u32[]{:S(2)}, u32[]{:S(2)}) %all-to-all-start) | async-done | bytes 8388640 | tf_op jit(solution)/shard_map/all_to_all | solution.py:145
  299.3 3.6 dynamic-slice_reduce_fusion
  305.4 139.7 %while.22 = (s32[]{:T(128)}, f32[64,1024]{1,0:T(8,128)}, s32[]{:T(128)}, s32[]{:T(128)}, f32[2,64,64]{2,1,0:T(8,128)}, /*index=5*/s32[128]{0:T(128)}, f32[64,102...) while((s32[]{:T(128)}, f32[64,1024]{1,0:T(8,128)}, ...), condition=%wide.region_2.4_spmd.clone, body=%wide.region_1.3_spmd.clone.sunk | while | flops 1613835264 | bytes 16157119 | solution.py:85
  325.3 3.4 fusion.197
  448.7 136.3 %while.23 = (s32[]{:T(128)}, f32[64,1024]{1,0:T(8,128)}, s32[]{:T(128)}, s32[]{:T(128)}, f32[2,64,64]{2,1,0:T(8,128)}, /*index=5*/s32[128]{0:T(128)S(1)}, f32[64...) while((s32[]{:T(128)}, f32[64,1024]{1,0:T(8,128)}, ...), condition=%wide.region_4.6_spmd.clone, body=%wide.region_3.5_spmd.clone.sunk | while | flops 1613835264 | bytes 16157119 | solution.py:85
  468.2 3.4 fusion.216
  490.9 3.4 fusion.216
  513.6 3.4 fusion.216
  536.2 3.4 fusion.216
  558.9 3.4 fusion.216
  581.6 3.4 fusion.216
  587.0 99.7 %all_to_all.36 = bf16[1,1,2,8,64,128]{5,3,2,1,0,4:T(8,128)(2,1)S(1)} all-to-all(bf16[1,1,2,8,64,128]{5,3,2,1,0,4:T(8,128)(2,1)S(1)} %copy.200), channel_id=1, replica_groups=mesh['slab'=8,'col'=16] {'slab'}, dimensions={4} | all-to-all | bytes 524288 | tf_op jit(solution)/shard_map/all_to_all | solution.py:158
  687.6 38.0 %all-gather.3.cloned.1.call-done = bf16[8,16,1,2,8,8,128]{6,5,4,3,2,0,1:T(8,128)(2,1)} async-done(((bf16[8,1,1,2,8,8,128]{6,5,4,3,2,0,1:T(8,128)(2,1)}), bf16[8,16,1,2,8,8,128]{6,5,4,3,2,0,1:T(8,128)(2,1)}) %all-gather.3.cloned.1.call-update) | async-done | bytes 4194320 | tf_op jit(solution)/shard_map/all_gather | solution.py:161
  728.9 12.5 %convert_bitcast_fusion = bf16[128,8,8,128]{3,1,2,0:T(8,128)(2,1)S(1)} fusion(bf16[256,8,8,128]{3,2,1,0:T(8,128)(2,1)S(1)} %bitcast.260, s32[2048]{0:T(1024)S(1)} %bitcast.268, s32[2048]{0:T(1024)S(1)} %bitcast.270, s32[2048]{0:T(1024)S(1)} %bitcast.272, s32[2048]{0:T(1024)S(1)} %bitcast.274, s32[2048]{0:T(1024)S(1)} %bitcast.276, s32[2048]{0:T(1024)S(1)} %bitcast.278, ...), kind=kOutput, calls=%fused_computation.166 | convolution fusion | flops 4363124736 | bytes 6356992 | tf_op jit(solution)/shard_map/dot_general | solution.py:164
  (375 shorter events, 277.4 us)
Async XLA Ops:
  6.5 184.9 %all-reduce.2.cloned.1.call-start = ((), (), s32[]{:S(2)}) async-start(), calls=%async_computation.2 | async-start | bytes 16777216 | tf_op jit(solution)/shard_map/psum | solution.py:144
  8.4 5.3 copy-start.6
  8.5 5.3 copy-start.8
  8.5 5.3 copy-start.10
  8.5 5.3 copy-start.12
  8.5 5.3 copy-start.14
  8.5 5.3 copy-start.16
  8.5 5.3 copy-start.18
  199.3 6.5 copy-start.1
  199.3 100.1 %all-to-all-start = ((f32[8,8,16,2048]{3,2,0,1:T(8,128)}), f32[8,8,16,2048]{3,2,0,1:T(8,128)}, u32[]{:S(2)}, u32[]{:S(2)}) async-start(f32[8,8,16,2048]{3,2,0,1:T(8,128)} %copy.195), calls=%async_computation | async-start | bytes 16777216 | tf_op jit(solution)/shard_map/all_to_all | solution.py:145
  205.7 520.0 %all-gather.3.cloned.1.call-start = ((), (), s32[]{:S(2)}) async-start(), calls=%async_computation.3 | async-start | bytes 4456448 | tf_op jit(solution)/shard_map/all_gather | solution.py:161
  319.3 5.1 copy-start.2
  342.6 5.1 copy-start.2
  389.2 5.1 copy-start.2
  412.5 5.1 copy-start.2
  435.8 5.1 copy-start.2
  507.5 5.1 copy-start.3
  687.5 41.3 %copy-start.7 = (s32[2048,1]{0,1:T(1,128)S(1)}, s32[2048,1]{0,1:T(1,128)}, u32[]{:S(2)}) copy-start(s32[2048,1]{0,1:T(1,128)} %copy-done.6) | copy-start | bytes 24580
  687.5 41.3 %copy-start.9 = (s32[2048,1]{0,1:T(1,128)S(1)}, s32[2048,1]{0,1:T(1,128)}, u32[]{:S(2)}) copy-start(s32[2048,1]{0,1:T(1,128)} %copy-done.8) | copy-start | bytes 24580
  687.6 41.3 %copy-start.11 = (s32[2048,1]{0,1:T(1,128)S(1)}, s32[2048,1]{0,1:T(1,128)}, u32[]{:S(2)}) copy-start(s32[2048,1]{0,1:T(1,128)} %copy-done.10) | copy-start | bytes 24580
  687.6 41.3 %copy-start.13 = (s32[2048,1]{0,1:T(1,128)S(1)}, s32[2048,1]{0,1:T(1,128)}, u32[]{:S(2)}) copy-start(s32[2048,1]{0,1:T(1,128)} %copy-done.12) | copy-start | bytes 24580
  687.6 41.3 %copy-start.15 = (s32[2048,1]{0,1:T(1,128)S(1)}, s32[2048,1]{0,1:T(1,128)}, u32[]{:S(2)}) copy-start(s32[2048,1]{0,1:T(1,128)} %copy-done.14) | copy-start | bytes 24580
  687.6 41.3 %copy-start.17 = (s32[2048,1]{0,1:T(1,128)S(1)}, s32[2048,1]{0,1:T(1,128)}, u32[]{:S(2)}) copy-start(s32[2048,1]{0,1:T(1,128)} %copy-done.16) | copy-start | bytes 24580
  687.6 41.3 %copy-start.19 = (s32[2048,1]{0,1:T(1,128)S(1)}, s32[2048,1]{0,1:T(1,128)}, u32[]{:S(2)}) copy-start(s32[2048,1]{0,1:T(1,128)} %copy-done.18) | copy-start | bytes 24580
  (9 other events, 37.6 us)
Sparse Core Ops, SparseCore 0:
  47.0 144.4 all-reduce.1
  687.7 37.9 all-gather.2
where the time goes:
time: 771 us; the launch traced here: 757 us
  waiting for transfers between devices  255 us (33%)
  local copies, waits for them, and re-layouts  157 us (20%)
  matrix products  140 us (18%)
  blocking collectives  99.7 us (13%)
  other arithmetic  82 us (11%)
  between operations  15.5 us (2%)
    psum x1, waiting for transfers between devices, on_device(): summed = lax.psum(partial_value, 'col')  145 us
    all_to_all x1, blocking collectives, on_device(): lax.all_to_all(outgoing, 'slab', split_axis=4, concat_axis=0, tiled=True)  99.7 us
    all_to_all x1, waiting for transfers between devices, on_device(): lax.all_to_all(summed, 'slab', split_axis=1, concat_axis=0, tiled=True)  72.6 us
    dot_general x48, matrix products, along_last(): result = jnp.matmul(stacked, dft_table, precision=lax.Precision.HIGHEST)  64.1 us
    gather x24, local copies, waits for them, and re-layouts, block_step(): jnp.take(phase_image, columns, axis=1)  44.3 us
    dot_general x12, matrix products, block_step(): jnp.dot(flat_grad, placement, precision=lax.Precision.HIGHEST)  40.5 us
    all_gather x1, waiting for transfers between devices, on_device(): lax.all_gather(incoming, 'col', axis=1, tiled=True)  38 us
    sin x12, other arithmetic, block_step(): sine_part = jnp.sin(patch_phase)  30.3 us
  transfers between devices with their start and end apart: 3, of which 3 were waited for; matrix products, arithmetic and copies ran while one was open for 3% of the time, Pallas kernels for 0%

commit v1 on v0

v1 whole, which is shorter than its diff:
```python
import functools
import math

import jax
import jax.numpy as jnp
import numpy as np
from jax import lax
from jax.experimental import pallas as pl
from jax.experimental.pallas import tpu as pltpu
from jax.sharding import PartitionSpec as P

BF16 = jnp.bfloat16
F32 = jnp.float32
GROUP = 8
step_size = 0.1
penalty = 1.0


def trig_coefficients():
    grid = (np.cos(np.pi * (np.arange(400) + 0.5) / 400) + 1.0) * (np.pi * np.pi * 0.5005)
    root = np.sqrt(grid)
    sine = np.polynomial.Polynomial.fit(grid, np.sin(root) / root, 6).convert().coef
    cosine = np.polynomial.Polynomial.fit(grid, np.cos(root), 7).convert().coef
    return [float(v) for v in sine], [float(v) for v in cosine]


def sine_cosine(angle):
    sine, cosine = trig_coefficients()
    square = angle * angle
    sine_value = jnp.full_like(square, sine[-1])
    for value in sine[-2::-1]:
        sine_value = sine_value * square + value
    cosine_value = jnp.full_like(square, cosine[-1])
    for value in cosine[-2::-1]:
        cosine_value = cosine_value * square + value
    return sine_value * angle, cosine_value


def split_bf16(table):
    high = table.astype(np.float32).astype(BF16)
    low = (table - high.astype(np.float64)).astype(np.float32).astype(BF16)
    return high, low


def transform_tables(size):
    index = np.arange(size)
    radians = 2.0 * np.pi / size * (index[:, None] * index[None, :] % size)
    cosine = np.cos(radians) / math.sqrt(size)
    sine = np.sin(radians) / math.sqrt(size)
    zero = np.zeros_like(cosine)
    forward = np.block([[cosine, -sine], [sine, cosine]])
    pair = np.block([[cosine, zero, sine, zero], [zero, cosine, zero, sine]])
    back = np.block([[2 * sine, -2 * cosine], [2 * cosine, 2 * sine]])
    f_high, f_low = split_bf16(forward)
    p_high, p_low = split_bf16(pair)
    b_high, b_low = split_bf16(back)
    lanes = np.concatenate([f_high, f_low], 1)
    return (
        np.concatenate([lanes, lanes], 0),
        np.concatenate([p_high, p_high], 0),
        p_low,
        np.concatenate([b_high, b_low], 1),
    )


def halves(value):
    high = value.astype(BF16)
    low = (value - high.astype(F32)).astype(BF16)
    return high, low


def dot(left, right):
    return jnp.dot(left, right, preferred_element_type=F32)


def ptycho_kernel(
    counts, starts, image, probe_a, probe_b, t_first, t_pair, t_pair_low, t_back, measured,
    out, waves, total, staged, observed,
):
    slots, size, _, limit = measured.shape
    width = waves.shape[0]
    tile = image.shape[1]
    rows = width // tile * slots
    chunk_count = limit // GROUP

    def used_chunks(slot):
        return jnp.clip(lax.div(counts[slot] + (GROUP - 1), GROUP), 0, chunk_count)

    half = size // 2

    @pl.loop(0, slots)
    def _(slot):
        for row in range(half):
            both = jnp.concatenate([measured[slot, row], measured[slot, row + half]], 0)
            observed[slot, pl.ds(row, limit, half), :] = both.T

    staged[...] = image[...].astype(jnp.int32).astype(F32) * (2 * math.pi / 65536)
    lane = lax.broadcasted_iota(jnp.int32, (size, 2 * size), 1)

    @pl.loop(0, slots)
    def _(slot):
        for part in range(width // tile):
            sine, cosine = sine_cosine(staged[pl.ds(slot * (width // tile) + part, size, rows), :])
            waves[part * tile : (part + 1) * tile, :] = jnp.concatenate([cosine, sine], 0).T
        total[...] = jnp.zeros_like(total)
        count = counts[slot]

        @pl.loop(0, used_chunks(slot))
        def _(chunk):
            begin = chunk * GROUP
            at = [starts[slot, begin + member] for member in range(GROUP)]
            exits = []
            for member in range(GROUP):
                patch = waves[pl.ds(at[member], size), :]
                exits.append(probe_a[...] * patch + probe_b[...] * pltpu.roll(patch, size, 1))
            exit_wave = jnp.concatenate(exits, 0)
            high, low = halves(exit_wave)
            first = dot(jnp.concatenate([high, low], 1), t_first[...])
            first = first[:, : 2 * size] + first[:, 2 * size :]
            turned = jnp.concatenate(
                [first[pair * 2 * size : (pair + 1) * 2 * size].T for pair in range(GROUP // 2)], 0
            )
            high, low = halves(turned)
            second = dot(jnp.concatenate([high, low], 1), t_pair[...])
            second = second + dot(high, t_pair_low[...])
            scaled = []
            for pair in range(GROUP // 2):
                block = second[pair * 2 * size : (pair + 1) * 2 * size]
                real = block[:size, : 2 * size] + block[size:, 2 * size :]
                imag = block[size:, : 2 * size] - block[:size, 2 * size :]
                member = begin + 2 * pair
                seen = [
                    observed[slot, pl.ds(pl.multiple_of((member + m) * half, half), half), :]
                    for m in range(2)
                ]
                seen = jnp.concatenate(
                    [
                        jnp.concatenate([seen[0][:, :size], seen[1][:, :size]], 1),
                        jnp.concatenate([seen[0][:, size:], seen[1][:, size:]], 1),
                    ],
                    0,
                )
                residual = real * real + imag * imag - seen
                live = member + jnp.where(lane >= size, 1, 0) < count
                residual = jnp.where(live, residual, 0.0)
                scaled += [residual * real, residual * imag]
            third = dot(jnp.concatenate(scaled, 0).astype(BF16), t_pair[: 2 * size, :])
            turned = []
            for pair in range(GROUP // 2):
                block = third[pair * 2 * size : (pair + 1) * 2 * size]
                real = block[:size, : 2 * size] - block[size:, 2 * size :]
                imag = block[size:, : 2 * size] + block[:size, 2 * size :]
                turned.append(jnp.concatenate([real, imag], 0).T)
            back = dot(jnp.concatenate(turned, 0).astype(BF16), t_back[...])
            gradient = exit_wave * (back[:, : 2 * size] + back[:, 2 * size :])
            for member in range(GROUP):
                span = pl.ds(at[member], size)
                total[span, :] = total[span, :] + gradient[member * size : (member + 1) * size]

        for part in range(width // tile):
            flat = total[part * tile : (part + 1) * tile, :].T
            staged[pl.ds(slot * (width // tile) + part, size, rows), :] = flat[:size] + flat[size:]

    out[...] = staged[...].astype(BF16)


def ptycho(image, probe_wave, measured, counts, starts):
    slots, size, _, limit = measured.shape
    height, tile = image.shape
    width = height // size // slots * tile
    tables = [jnp.asarray(table) for table in transform_tables(size)]
    turned = jnp.swapaxes(probe_wave, 1, 2)
    probe_a = jnp.concatenate([turned[0], turned[0]], 1)
    probe_b = jnp.concatenate([-turned[1], turned[1]], 1)
    scalar = pl.BlockSpec(memory_space=pltpu.SMEM)
    vector = pl.BlockSpec(memory_space=pltpu.VMEM)
    return pl.pallas_call(
        ptycho_kernel,
        out_shape=jax.ShapeDtypeStruct((height, tile), BF16),
        in_specs=[scalar, scalar] + [vector] * 8,
        out_specs=vector,
        scratch_shapes=[
            pltpu.VMEM((width, 2 * size), F32),
            pltpu.VMEM((width, 2 * size), F32),
            pltpu.VMEM((height, tile), F32),
            pltpu.VMEM((slots, limit * size // 2, 2 * size), F32),
        ],
        compiler_params=pltpu.CompilerParams(vmem_limit_bytes=48 * 2**20),
        cost_estimate=pl.CostEstimate(
            flops=2**34, bytes_accessed=2**23, transcendentals=0
        ),
    )(counts, starts, image, probe_a, probe_b, *tables, measured)


TURN = 65536 / (2 * math.pi)


def project_kernel(volume, templates, pattern, out, flat, table, counts, index):
    slab_rows, cells = volume.shape
    group, tile_cells, tile = templates.shape
    tiles = cells // tile_cells
    spread = pattern.shape[1]
    columns, _, slabs = out.shape[:3]
    step = 32
    for base in range(0, tiles, step):
        left = jnp.concatenate(
            [
                volume[:, t * tile_cells : (t + 1) * tile_cells].astype(F32)
                for t in range(base, base + step)
            ],
            0,
        ).astype(BF16)
        for k in range(0, group, 2):
            right = jnp.concatenate([templates[k], templates[k + 1]], 1)
            result = dot(left, right)
            span = slice(base * slab_rows, (base + step) * slab_rows)
            flat[k, span, :] = result[:, :tile]
            flat[k + 1, span, :] = result[:, tile:]
    for k in range(group):
        for z in range(slab_rows):
            block = flat[k, pl.ds(z, tiles, slab_rows), :]
            table[k * tiles : (k + 1) * tiles, z * tile : (z + 1) * tile] = block.astype(BF16)

    angles = pattern.shape[2]
    own = angles * pattern.shape[0] // (columns * slabs)
    turned = jnp.concatenate(
        [
            pattern[:, :, base : base + tile].reshape(-1, tile).T
            for base in range(0, angles, tile)
        ],
        0,
    )
    turned = (turned & (group - 1)) * tiles + lax.shift_right_logical(turned, 3)
    for d in range(pattern.shape[0]):
        index[pl.ds(d, angles, pattern.shape[0]), :spread] = turned[:, d * spread : (d + 1) * spread]

    lane = lax.broadcasted_iota(jnp.int32, (2 * slabs * own, tiles), 1)

    @pl.loop(0, columns // 2)
    def _(chip):
        wanted = jnp.concatenate(
            [
                index[pl.ds(pl.multiple_of((s * columns + 2 * chip + core) * own, own), own), :]
                for core in range(2)
                for s in range(slabs)
            ],
            0,
        )
        for k in range(group):
            held = jnp.zeros(lane.shape, F32)
            for member in range(spread):
                held = held + jnp.where(wanted[:, member : member + 1] == lane + k * tiles, 1.0, 0.0)
            counts[:, k * tiles : (k + 1) * tiles] = held.astype(BF16)
        for z in range(0, slab_rows, 2):
            result = dot(counts[...], table[:, z * tile : (z + 2) * tile])
            result = jnp.floor(result * TURN + 0.5).astype(jnp.int32).astype(jnp.int16)
            for core in range(2):
                for more in range(2):
                    block = result[
                        core * slabs * own : (core + 1) * slabs * own,
                        more * tile : (more + 1) * tile,
                    ]
                    out[2 * chip + core, z + more] = block.reshape(slabs, own, tile)


def project(volume, templates, pattern, columns, slabs):
    slab_rows, cells = volume.shape
    group, tile_cells, tile = templates.shape
    tiles = cells // tile_cells
    tile_rows, spread, angles = pattern.shape
    rows = angles * tile_rows
    own = rows // (columns * slabs)
    vector = pl.BlockSpec(memory_space=pltpu.VMEM)
    return pl.pallas_call(
        project_kernel,
        out_shape=jax.ShapeDtypeStruct((columns, slab_rows, slabs, own, tile), jnp.int16),
        in_specs=[vector] * 3,
        out_specs=vector,
        scratch_shapes=[
            pltpu.VMEM((group, tiles * slab_rows, tile), F32),
            pltpu.VMEM((group * tiles, slab_rows * tile), BF16),
            pltpu.VMEM((2 * slabs * own, group * tiles), BF16),
            pltpu.VMEM((rows, tile), jnp.int32),
        ],
        compiler_params=pltpu.CompilerParams(vmem_limit_bytes=48 * 2**20),
    )(volume, templates, pattern)


def spread_kernel(
    step_size, penalty,
    gathered, pattern, templates, volume, consensus, out, grads, counts, flat,
):
    columns, slabs, slab_rows, own, tile = gathered.shape
    spread, rows = pattern.shape
    group, tile_cells, _ = templates.shape
    tiles = flat.shape[1] // slab_rows
    here = volume.shape[1] // tile_cells

    @pl.when(pl.program_id(0) == 0)
    def _():
        for z in range(slab_rows):
            grads[:, z * tile : (z + 1) * tile] = gathered[:, :, z].reshape(rows, tile)

        chunk = tiles
        row = lax.broadcasted_iota(jnp.int32, (chunk, 256), 0)

        @pl.loop(0, group)
        def _(k):
            for base in range(0, rows, 256):
                entry = pattern[:, base : base + 256]
                wanted = (entry & (group - 1)) * tiles + lax.shift_right_logical(entry, 3)
                held = jnp.zeros((chunk, 256), F32)
                for member in range(spread):
                    held = held + jnp.where(
                        wanted[member : member + 1, :] == row + k * tiles, 1.0, 0.0
                    )
                counts[pl.ds(pl.multiple_of(k * tiles, tiles), tiles), base : base + 256] = (
                    held.astype(BF16)
                )

        for base in range(0, group, 2):
            for z in range(0, slab_rows, 2):
                result = dot(
                    counts[base * tiles : (base + 2) * tiles, :],
                    grads[:, z * tile : (z + 2) * tile],
                )
                result = result.astype(BF16).astype(F32)
                for k in range(2):
                    for more in range(2):
                        flat[base + k, pl.ds(z + more, tiles, slab_rows), :] = (
                            result[k * tiles : (k + 1) * tiles, more * tile : (more + 1) * tile]
                        )

    size = here * slab_rows
    mine = pl.ds(pl.multiple_of(pl.program_id(0) * size, size), size)
    left = jnp.concatenate([flat[k, mine, :] for k in range(group)], 1).astype(BF16)
    for part in range(0, tile_cells, 256):
        total = jnp.zeros((size, 256), F32)
        for k in range(0, group, 2):
            right = jnp.concatenate(
                [templates[k, part : part + 256, :], templates[k + 1, part : part + 256, :]], 1
            )
            total = total + lax.dot_general(
                left[:, k * tile : (k + 2) * tile],
                right,
                (((1,), (1,)), ((), ())),
                preferred_element_type=F32,
            )
        for t in range(here):
            span = slice(t * tile_cells + part, t * tile_cells + part + 256)
            own_volume = volume[:, span].astype(F32)
            wanted = consensus[:, span].astype(F32)
            moved = total[t * slab_rows : (t + 1) * slab_rows]
            out[:, span] = own_volume - step_size * (moved + penalty * (own_volume - wanted))


def spread_back(gathered, pattern_columns, templates, volume, consensus, step_size, penalty):
    slab_rows, cells = volume.shape
    group, tile_cells, tile = templates.shape
    tiles = cells // tile_cells
    rows = pattern_columns.shape[1]
    vector = pl.BlockSpec(memory_space=pltpu.VMEM)
    steps = 4
    block = pl.BlockSpec((slab_rows, cells // steps), lambda i: (0, i))
    return pl.pallas_call(
        functools.partial(spread_kernel, step_size, penalty),
        grid=(steps,),
        out_shape=jax.ShapeDtypeStruct((slab_rows, cells), F32),
        in_specs=[vector] * 3 + [block, block],
        out_specs=block,
        scratch_shapes=[
            pltpu.VMEM((rows, slab_rows * tile), BF16),
            pltpu.VMEM((group * tiles, rows), BF16),
            pltpu.VMEM((group, tiles * slab_rows, tile), F32),
        ],
        compiler_params=pltpu.CompilerParams(vmem_limit_bytes=48 * 2**20),
    )(gathered, pattern_columns, templates, volume, consensus)


def steps_over():
    return [(dx, dy) for dx in range(2) for dy in range(4)]


def moved(index, step):
    high, low = lax.div(index, 4), lax.rem(index, 4)
    return lax.rem(high + step[0], 2) * 4 + lax.rem(low + step[1], 4)


def greet(slab, chip, core):
    barrier = pltpu.get_barrier_semaphore()
    here = slab, 2 * chip + core
    others = [(slab, 2 * chip + 1 - core)]
    others += [(slab, 2 * moved(chip, step) + core) for step in steps_over()[1:]]
    others += [(moved(slab, step), here[1]) for step in steps_over()[1:]]
    for other in others:
        pl.semaphore_signal(barrier, inc=1, device_id=other, device_id_type=pl.DeviceIdType.MESH)
    pl.semaphore_wait(barrier, len(others))


def remote(source, target, send, receive, device):
    return pltpu.make_async_remote_copy(
        src_ref=source,
        dst_ref=target,
        send_sem=send,
        recv_sem=receive,
        device_id=device,
        device_id_type=pl.DeviceIdType.MESH,
    )


def reduce_kernel(
    partial, out, own, pair, sent, arrived, total,
    own_sem, pair_send, pair_recv, chip_send, chip_recv, slab_send, slab_recv,
):
    slab, column = lax.axis_index("slab"), lax.axis_index("col")
    chip, core = lax.div(column, 2), lax.rem(column, 2)
    slabs, slab_rows = out.shape[:2]
    steps = steps_over()
    order = list(range(1, 8)) + [0]
    greet(slab, chip, core)

    locals_, pairs, chips, slabs_ = {}, {}, {}, {}
    for d in order:
        target = 2 * moved(chip, steps[d])
        pairs[d] = remote(
            partial.at[target + 1 - core], pair.at[d], pair_send.at[d], pair_recv.at[d],
            (slab, 2 * chip + 1 - core),
        )
        pairs[d].start()
        locals_[d] = pltpu.make_async_copy(partial.at[target + core], own.at[d], own_sem.at[d])
        locals_[d].start()
    for d in order:
        locals_[d].wait()
        pairs[d].wait_recv()
        if d:

            @pl.loop(0, slab_rows)
            def _(z):
                sent[d, z] = own[d, z] + pair[d, z]

            chips[d] = remote(
                sent.at[d], arrived.at[d], chip_send.at[d], chip_recv.at[d],
                (slab, 2 * moved(chip, steps[d]) + core),
            )
            chips[d].start()
    for d in order[:-1]:
        chips[d].wait_recv()

    @pl.loop(0, slab_rows)
    def _(z):
        value = own[0, z] + pair[0, z]
        for d in range(1, 8):
            value = value + arrived[d, z]
        total[:, z] = value

    for d in order[:-1]:
        other = moved(slab, steps[d])
        slabs_[d] = remote(
            total.at[other], out.at[slab], slab_send.at[d], slab_recv.at[d], (other, column)
        )
        slabs_[d].start()
    out[slab] = total[slab]
    for d in order:
        pairs[d].wait_send()
    for d in order[:-1]:
        chips[d].wait_send()
        slabs_[d].wait()


def reduce_images(partial):
    columns, slab_rows, slabs, own, tile = partial.shape
    block = (8, slab_rows, slabs, own, tile)
    sem = pltpu.SemaphoreType.DMA((8,))
    return pl.pallas_call(
        reduce_kernel,
        out_shape=jax.ShapeDtypeStruct((slabs, slab_rows, own, tile), jnp.int16),
        in_specs=[pl.BlockSpec(memory_space=pl.ANY)],
        out_specs=pl.BlockSpec(memory_space=pltpu.VMEM),
        scratch_shapes=[pltpu.VMEM(block, jnp.int16)] * 4
        + [pltpu.VMEM((slabs, slab_rows, own, tile), jnp.int16)]
        + [sem] * 7,
        compiler_params=pltpu.CompilerParams(
            collective_id=1, has_side_effects=True, vmem_limit_bytes=32 * 2**20
        ),
    )(partial)


def gather_kernel(
    grads, out, mine, held, slab_send, slab_recv, chip_send, chip_recv, pair_send, pair_recv,
    out_sem,
):
    slab, column = lax.axis_index("slab"), lax.axis_index("col")
    chip, core = lax.div(column, 2), lax.rem(column, 2)
    sibling = (slab, 2 * chip + 1 - core)
    steps = steps_over()
    greet(slab, chip, core)

    slabs_, chips, pairs, locals_ = {}, {}, {}, {}
    for d in range(1, 8):
        other = moved(slab, steps[d])
        slabs_[d] = remote(
            grads.at[other], mine.at[slab], slab_send.at[d], slab_recv.at[d], (other, column)
        )
        slabs_[d].start()
    mine[slab] = grads[slab]
    for d in range(1, 8):
        slabs_[d].wait_recv()
    for d in range(1, 8):
        target = moved(chip, steps[d])
        chips[d] = remote(
            mine, held.at[d], chip_send.at[d], chip_recv.at[d], (slab, 2 * target + core)
        )
        chips[d].start()
    for d in range(8):
        if d:
            chips[d].wait_recv()
        source = mine if d == 0 else held.at[d]
        origin = moved(chip, ((2 - steps[d][0]) % 2, (4 - steps[d][1]) % 4))
        place = out.at[2 * origin + core]
        pairs[d] = remote(source, place, pair_send.at[d], pair_recv.at[d], sibling)
        pairs[d].start()
        locals_[d] = pltpu.make_async_copy(source, place, out_sem.at[d])
        locals_[d].start()
    for d in range(8):
        locals_[d].wait()
        pairs[d].wait()
        if d:
            chips[d].wait_send()
            slabs_[d].wait_send()


def gather_grads(grads):
    slabs, slab_rows, own, tile = grads.shape
    sem = pltpu.SemaphoreType.DMA((8,))
    return pl.pallas_call(
        gather_kernel,
        out_shape=jax.ShapeDtypeStruct((16, slabs, slab_rows, own, tile), BF16),
        in_specs=[pl.BlockSpec(memory_space=pltpu.VMEM)],
        out_specs=pl.BlockSpec(memory_space=pl.ANY),
        scratch_shapes=[pltpu.VMEM(grads.shape, BF16), pltpu.VMEM((8,) + grads.shape, BF16)]
        + [sem] * 7,
        compiler_params=pltpu.CompilerParams(
            collective_id=2, has_side_effects=True, vmem_limit_bytes=32 * 2**20
        ),
    )(grads)


def on_device(
    volume, consensus, templates, pattern, probe_wave, measured, scan_counts, scan_positions
):
    slab_rows = volume.shape[0]
    tile = templates.shape[2]
    slab_count = lax.axis_size("slab")
    column_count = lax.axis_size("col")
    angle_count, tile_rows, spread = pattern.shape[1:]
    per_owner = angle_count // (slab_count * column_count)
    own = per_owner * tile_rows
    rows = angle_count * tile_rows
    owner = lax.axis_index("slab") * column_count + lax.axis_index("col")
    counts = lax.dynamic_slice_in_dim(scan_counts, owner * per_owner, per_owner)
    starts = lax.dynamic_slice_in_dim(scan_positions, owner * per_owner, per_owner)

    partial = project(
        volume, templates, pattern[0].transpose(1, 2, 0), column_count, slab_count
    )
    image = reduce_images(partial).reshape(slab_count * slab_rows * own, tile)

    gradients = ptycho(image, probe_wave, measured.transpose(0, 2, 3, 1), counts, starts)

    gathered = gather_grads(gradients.reshape(slab_count, slab_rows, own, tile))
    pattern_columns = pattern.reshape(slab_count, column_count, own, spread)
    pattern_columns = pattern_columns.transpose(3, 1, 0, 2).reshape(spread, rows)
    return spread_back(
        gathered, pattern_columns, templates, volume, consensus, step_size, penalty
    )


def solution(mesh):
    return jax.shard_map(
        on_device,
        mesh=mesh,
        in_specs=(
            P("slab", "col"),
            P("slab", "col"),
            P("col", None, None),
            P("col", None, None, None),
            P(),
            P(("slab", "col"), None, None, None),
            P(),
            P(),
        ),
        out_specs=P("slab", "col"),
        check_vma=False,
    )
```

time: 771 us -> 167 us (0.22); the launches traced: 757 us -> 167 us
  waiting for transfers between devices: 255 us -> 0 us
  Pallas kernels: 0 us -> 155 us
  local copies, waits for them, and re-layouts: 157 us -> 11.2 us
  matrix products: 140 us -> 0 us
  blocking collectives: 99.7 us -> 0 us
  other arithmetic: 82 us -> 0.09 us
  between operations: 15.5 us -> 0.16 us
    pallas_call x0 -> x5, Pallas kernels: none -> 155 us  [the longest x1 42.9 us: gather_grads(): pl.pallas_call(gather_kernel, out_shape=jax.ShapeDtypeStruct((16, slabs,...]
    psum x1 -> x0, waiting for transfers between devices: 145 us -> none  [on_device(): summed = lax.psum(partial_value, 'col')]
    dot_general x64 -> x0, matrix products: 140 us -> none  [the longest x48 64.1 us: along_last(): result = jnp.matmul(stacked, dft_table, precision=lax.Precision.HIGHEST)]
    all_to_all x1 -> x0, blocking collectives: 99.7 us -> none  [on_device(): lax.all_to_all(outgoing, 'slab', split_axis=4, concat_axis=0, tiled=True)]
    all_to_all x1 -> x0, waiting for transfers between devices: 72.6 us -> none  [on_device(): lax.all_to_all(summed, 'slab', split_axis=1, concat_axis=0, tiled=True)]
    gather x26 -> x0, local copies, waits for them, and re-layouts: 46.4 us -> none  [the longest x24 44.3 us: block_step(): jnp.take(phase_image, columns, axis=1)]
    all_gather x1 -> x0, waiting for transfers between devices: 38 us -> none  [on_device(): lax.all_gather(incoming, 'col', axis=1, tiled=True)]
    sin x12 -> x0, other arithmetic: 30.3 us -> none  [block_step(): sine_part = jnp.sin(patch_phase)]
  transfers between devices with their start and end apart: 3 -> 0, of which waited for: 3 -> 0; matrix products, arithmetic and copies ran while one was open for 3% -> 0% of each run, Pallas kernels for 0% -> 0%
where the time goes in v1:
time: 167 us
  Pallas kernels  155 us (93%)
  local copies, waits for them, and re-layouts  11.2 us (7%)
    pallas_call x1, Pallas kernels, gather_grads(): pl.pallas_call(gather_kernel, out_shape=jax.ShapeDtypeStruct((16, slabs,...  42.9 us
    pallas_call x1, Pallas kernels, reduce_images(): pl.pallas_call(reduce_kernel, out_shape=jax.ShapeDtypeStruct((slabs, slab...  41.7 us
    pallas_call x1, Pallas kernels, ptycho(): pl.pallas_call(ptycho_kernel, out_shape=jax.ShapeDtypeStruct((height, til...  31.1 us
    pallas_call x1, Pallas kernels, project(): pl.pallas_call(project_kernel, out_shape=jax.ShapeDtypeStruct((columns, s...  20.1 us
    pallas_call x1, Pallas kernels, spread_back(): pl.pallas_call(functools.partial(spread_kernel, step_size, penalty), grid...  19.7 us
    unnamed x26, local copies, waits for them, and re-layouts  7.85 us

profile of v1, /device:TPU:1, one launch (start us, length us, event | category | flops | bytes accessed | tf_op | source)
XLA Modules:
  0.0 167.0 jit_solution(1549065901000914343)
XLA Ops:
  0.0 0.0 copy-start
  0.0 0.9 dynamic_slice.6.counts
  0.9 0.0 copy-done
  0.9 0.9 copy.14
  1.9 0.1 pad_maximum_fusion
  2.0 1.2 copy.15
  3.2 1.0 reshape.14
  4.2 1.2 copy.16
  5.4 0.3 reshape.15.pattern
  5.6 0.0 copy-done.6
  5.6 0.0 copy-done.3
  5.7 0.0 copy-start.4
  5.7 1.6 copy-done.4
  7.3 20.1 %shard_map.118.partial = s16[16,8,8,16,128]{4,3,2,1,0:T(8,128)(2,1)} custom-call(bf16[8,131072]{1,0:T(8,128)(2,1)S(1)} %copy-done.3, bf16[8,1024,128]{2,1,0:T(8,128)(2,1)S(1)} %copy-done.4, s32[8,8,256]{2,1,0:T(8,128)S(1)} %bitcast.20), custom_call_target="tpu_custom_call" | custom-call | tf_op jit(solution)/shard_map/pallas_call | solution.py:274
  27.4 2.2 %copy-done.2 = s16[16,8,8,16,128]{4,3,2,1,0:T(8,128)(2,1)S(1)} copy-done((s16[16,8,8,16,128]{4,3,2,1,0:T(8,128)(2,1)S(1)}, s16[16,8,8,16,128]{4,3,2,1,0:T(8,128)(2,1)}, u32[]{:S(2)}) %copy-start.2) | copy-done | bytes 4194328
  29.6 41.7 %shard_map.119 = s16[8,8,16,128]{3,2,1,0:T(8,128)(2,1)S(1)} custom-call(s16[16,8,8,16,128]{4,3,2,1,0:T(8,128)(2,1)S(1)} %copy-done.2), custom_call_target="tpu_custom_call" | custom-call | tf_op jit(solution)/shard_map/pallas_call | solution.py:474
  71.2 0.0 copy-done.10
  71.3 0.0 copy-done.11
  71.3 0.0 copy-done.7
  71.3 31.1 %shard_map.120 = bf16[1024,128]{1,0:T(8,128)(2,1)S(1)} custom-call(s32[2]{0:T(128)S(1)} %dynamic_slice.6.counts, s32[2,128]{1,0:T(2,128)S(1)} %constant_dynamic-slice_fusion.starts, s16[1024,128]{1,0:T(8,128)(2,1)S(1)} %bitcast.21, f32[64,128]{1,0:T(8,128)S(1)} %get-tuple-element.7.probe_a, f32[64,128]{1,0:T(8,128)S(1)} %get-tuple-element.8.probe_b, ...), custom_call_target="tpu_custom_call" | custom-call | flops 17179869184 | bytes 8388608 | tf_op jit(solution)/shard_map/pallas_call | solution.py:177
  102.4 0.0 copy-start.5
  102.4 42.9 %shard_map.121.gathered = bf16[16,8,8,16,128]{4,3,2,1,0:T(8,128)(2,1)S(1)} custom-call(bf16[8,8,16,128]{3,2,1,0:T(8,128)(2,1)S(1)} %bitcast.22), custom_call_target="tpu_custom_call" | custom-call | tf_op jit(solution)/shard_map/pallas_call | solution.py:535
  145.4 1.9 %copy-done.1 = bf16[16,8,8,16,128]{4,3,2,1,0:T(8,128)(2,1)} copy-done((bf16[16,8,8,16,128]{4,3,2,1,0:T(8,128)(2,1)}, bf16[16,8,8,16,128]{4,3,2,1,0:T(8,128)(2,1)S(1)}, u32[]{:S(2)}) %copy-start.1) | copy-done | bytes 4194328
  147.3 19.7 %shard_map.122 = f32[8,131072]{1,0:T(8,128)} custom-call(bf16[16,8,8,16,128]{4,3,2,1,0:T(8,128)(2,1)} %copy-done.1, s32[8,2048]{1,0:T(8,128)S(1)} %reshape.15.pattern, bf16[8,1024,128]{2,1,0:T(8,128)(2,1)S(1)} %copy-done.5, bf16[8,131072]{1,0:T(8,128)(2,1)S(1)} %copy-done.3, bf16[8,131072]{1,0:T(8,128)(2,1)} %consensus.1), custom_call_target="tpu_custom_call" | custom-call | tf_op jit(solution)/shard_map/pallas_call | solution.py:365
  (15 shorter events, 0.0 us)
Async XLA Ops:
  0.0 0.9 copy-start
  0.0 5.6 %copy-start.6 = (s32[1,256,8,8]{1,3,2,0:T(8,128)S(1)}, s32[1,256,8,8]{1,3,2,0:T(8,128)}, u32[]{:S(2)}) copy-start(s32[1,256,8,8]{1,3,2,0:T(8,128)} %param.15) | copy-start | bytes 196612
  0.0 5.6 %copy-start.3 = (bf16[8,131072]{1,0:T(8,128)(2,1)S(1)}, bf16[8,131072]{1,0:T(8,128)(2,1)}, u32[]{:S(2)}) copy-start(bf16[8,131072]{1,0:T(8,128)(2,1)} %volume.3) | copy-start | bytes 6291460
  5.7 1.6 copy-start.4
  7.3 64.0 %copy-start.10 = (bf16[128,256]{1,0:T(8,128)(2,1)S(1)}, bf16[128,256]{1,0:T(8,128)(2,1)}, u32[]{:S(2)}) copy-start(bf16[128,256]{1,0:T(8,128)(2,1)} %constant.28.clone.t_back) | copy-start | bytes 196612
  7.3 64.0 %copy-start.11 = (bf16[128,256]{1,0:T(8,128)(2,1)S(1)}, bf16[128,256]{1,0:T(8,128)(2,1)}, u32[]{:S(2)}) copy-start(bf16[128,256]{1,0:T(8,128)(2,1)} %constant.27.clone.t_pair_low) | copy-start | bytes 196612
  27.4 2.2 %copy-start.2 = (s16[16,8,8,16,128]{4,3,2,1,0:T(8,128)(2,1)S(1)}, s16[16,8,8,16,128]{4,3,2,1,0:T(8,128)(2,1)}, u32[]{:S(2)}) copy-start(s16[16,8,8,16,128]{4,3,2,1,0:T(8,128)(2,1)} %shard_map.118.partial) | copy-start | bytes 12582916
  29.6 41.7 %copy-start.7 = (f32[2,128,64,64]{1,3,2,0:T(8,128)S(1)}, f32[2,128,64,64]{1,3,2,0:T(8,128)}, u32[]{:S(2)}) copy-start(f32[2,128,64,64]{1,3,2,0:T(8,128)} %param.17) | copy-start | bytes 12582916
  29.6 41.7 %copy-start.8 = (bf16[256,256]{1,0:T(8,128)(2,1)S(1)}, bf16[256,256]{1,0:T(8,128)(2,1)}, u32[]{:S(2)}) copy-start(bf16[256,256]{1,0:T(8,128)(2,1)} %constant.26.clone.t_pair) | copy-start | bytes 393220
  29.6 41.7 %copy-start.9 = (bf16[256,256]{1,0:T(8,128)(2,1)S(1)}, bf16[256,256]{1,0:T(8,128)(2,1)}, u32[]{:S(2)}) copy-start(bf16[256,256]{1,0:T(8,128)(2,1)} %constant.25.clone.t_first) | copy-start | bytes 393220
  102.4 44.9 %copy-start.5 = (bf16[8,1024,128]{2,1,0:T(8,128)(2,1)S(1)}, bf16[8,1024,128]{2,1,0:T(8,128)(2,1)}, u32[]{:S(2)}) copy-start(bf16[8,1024,128]{2,1,0:T(8,128)(2,1)} %templates.3) | copy-start | bytes 6291460
  145.4 1.9 %copy-start.1 = (bf16[16,8,8,16,128]{4,3,2,1,0:T(8,128)(2,1)}, bf16[16,8,8,16,128]{4,3,2,1,0:T(8,128)(2,1)S(1)}, u32[]{:S(2)}) copy-start(bf16[16,8,8,16,128]{4,3,2,1,0:T(8,128)(2,1)S(1)} %shard_map.121.gathered) | copy-start | bytes 12582916

commit v2 on v1

v2 whole, which is shorter than its diff:
```python
import functools
import math

import jax
import jax.numpy as jnp
import numpy as np
from jax import lax
from jax.experimental import pallas as pl
from jax.experimental.pallas import tpu as pltpu
from jax.sharding import PartitionSpec as P

BF16 = jnp.bfloat16
F32 = jnp.float32
GROUP = 8
step_size = 0.1
penalty = 1.0
I16 = jnp.int16
TURN = 65536 / (2 * math.pi)

def dot(left, right):
    return jnp.dot(left, right, preferred_element_type=F32)


def steps_over():
    return [(dx, dy) for dx in range(2) for dy in range(4)]


def moved(index, step):
    high, low = lax.div(index, 4), lax.rem(index, 4)
    return lax.rem(high + step[0], 2) * 4 + lax.rem(low + step[1], 4)


def greet_all(slab, chip, core):
    barrier = pltpu.get_barrier_semaphore()
    here = slab, 2 * chip + core
    others = [(slab, 2 * chip + 1 - core)]
    others += [(slab, 2 * moved(chip, step) + core) for step in steps_over()[1:]]
    others += [(moved(slab, step), here[1]) for step in steps_over()[1:]]
    for other in others:
        pl.semaphore_signal(barrier, inc=1, device_id=other, device_id_type=pl.DeviceIdType.MESH)


def greeted(number):
    pl.semaphore_wait(pltpu.get_barrier_semaphore(), number)


def remote(source, target, send, receive, device):
    return pltpu.make_async_remote_copy(
        src_ref=source,
        dst_ref=target,
        send_sem=send,
        recv_sem=receive,
        device_id=device,
        device_id_type=pl.DeviceIdType.MESH,
    )


def gather_kernel(
    grads, out, mine, held, slab_send, slab_recv, chip_send, chip_recv, pair_send, pair_recv,
    out_sem,
):
    slab, column = lax.axis_index("slab"), lax.axis_index("col")
    chip, core = lax.div(column, 2), lax.rem(column, 2)
    sibling = (slab, 2 * chip + 1 - core)
    steps = steps_over()
    greet_all(slab, chip, core)
    greeted(15)

    slabs_, chips, pairs, locals_ = {}, {}, {}, {}
    for d in range(1, 8):
        other = moved(slab, steps[d])
        slabs_[d] = remote(
            grads.at[other], mine.at[slab], slab_send.at[d], slab_recv.at[d], (other, column)
        )
        slabs_[d].start()
    mine[slab] = grads[slab]
    for d in range(1, 8):
        slabs_[d].wait_recv()
    for d in range(1, 8):
        target = moved(chip, steps[d])
        chips[d] = remote(
            mine, held.at[d], chip_send.at[d], chip_recv.at[d], (slab, 2 * target + core)
        )
        chips[d].start()
    for d in range(8):
        if d:
            chips[d].wait_recv()
        source = mine if d == 0 else held.at[d]
        origin = moved(chip, ((2 - steps[d][0]) % 2, (4 - steps[d][1]) % 4))
        place = out.at[2 * origin + core]
        pairs[d] = remote(source, place, pair_send.at[d], pair_recv.at[d], sibling)
        pairs[d].start()
        locals_[d] = pltpu.make_async_copy(source, place, out_sem.at[d])
        locals_[d].start()
    for d in range(8):
        locals_[d].wait()
        pairs[d].wait()
        if d:
            chips[d].wait_send()
            slabs_[d].wait_send()


def gather_grads(grads):
    slabs, slab_rows, own, tile = grads.shape
    sem = pltpu.SemaphoreType.DMA((8,))
    return pl.pallas_call(
        gather_kernel,
        out_shape=jax.ShapeDtypeStruct((16, slabs, slab_rows, own, tile), BF16),
        in_specs=[pl.BlockSpec(memory_space=pltpu.VMEM)],
        out_specs=pl.BlockSpec(memory_space=pl.ANY),
        scratch_shapes=[pltpu.VMEM(grads.shape, BF16), pltpu.VMEM((8,) + grads.shape, BF16)]
        + [sem] * 7,
        compiler_params=pltpu.CompilerParams(
            collective_id=2, has_side_effects=True, vmem_limit_bytes=32 * 2**20
        ),
    )(grads)


def segment_of(entry, group, tiles):
    return (entry & (group - 1)) * tiles + lax.div(entry, group)


def forward_kernel(
    volume_in, templates_in, pattern, measured_in, image, observed,
    volume, templates, measured, flat, table, counts, index, own, outgoing, pair, arrived, total,
    load_sem, pair_send, pair_recv, chip_send, chip_recv, slab_send, slab_recv,
):
    slab, column = lax.axis_index("slab"), lax.axis_index("col")
    chip, core = lax.div(column, 2), lax.rem(column, 2)
    slabs, slab_rows, share, tile = image.shape
    columns = 2 * own.shape[0]
    group, tile_cells, _ = templates.shape
    tiles = table.shape[0] // group
    tile_rows, spread, angles = pattern.shape
    half = measured.shape[1] // 2
    limit = measured.shape[3]
    quarter = volume.shape[1] // 4
    greet_all(slab, chip, core)

    loads = [pltpu.make_async_copy(templates_in, templates, load_sem.at[0])]
    for part in range(4):
        span = pl.ds(part * quarter, quarter)
        loads.append(
            pltpu.make_async_copy(volume_in.at[:, span], volume.at[:, span], load_sem.at[1 + part])
        )
    loads.append(pltpu.make_async_copy(measured_in, measured, load_sem.at[5]))
    for load in loads:
        load.start()

    turned = jnp.concatenate(
        [
            pattern[:, :, base : base + tile].reshape(-1, tile).T
            for base in range(0, angles, tile)
        ],
        0,
    )
    turned = segment_of(turned, group, tiles)
    for d in range(tile_rows):
        index[pl.ds(d, angles, tile_rows), :spread] = turned[:, d * spread : (d + 1) * spread]

    loads[0].wait()
    step = tiles // 4
    for part in range(4):
        loads[1 + part].wait()
        left = jnp.concatenate(
            [
                volume[:, t * tile_cells : (t + 1) * tile_cells].astype(F32)
                for t in range(part * step, (part + 1) * step)
            ],
            0,
        ).astype(BF16)
        span = slice(part * step * slab_rows, (part + 1) * step * slab_rows)
        for k in range(0, group, 2):
            result = dot(left, jnp.concatenate([templates[k], templates[k + 1]], 1))
            flat[k, span, :] = result[:, :tile]
            flat[k + 1, span, :] = result[:, tile:]
    for k in range(group):
        for z in range(slab_rows):
            block = flat[k, pl.ds(z, tiles, slab_rows), :]
            table[k * tiles : (k + 1) * tiles, z * tile : (z + 1) * tile] = block.astype(BF16)

    greeted(15)
    lane = lax.broadcasted_iota(jnp.int32, (2 * slabs * share, tiles), 1)

    def at_step(i):
        d = lax.rem(5 * i + 5, 8)
        high = lax.rem(lax.div(chip, 4) + lax.div(d, 4), 2)
        return d, 4 * high + lax.rem(chip + d, 4)

    def to_pair(d):
        return remote(
            outgoing.at[d], pair.at[d], pair_send.at[d], pair_recv.at[d],
            (slab, 2 * chip + 1 - core),
        )

    def to_chip(d, target):
        return remote(
            own.at[d], arrived.at[d], chip_send.at[d], chip_recv.at[d], (slab, 2 * target + core)
        )

    def compute(i):
        d, target = at_step(i)
        wanted = jnp.concatenate(
            [
                index[pl.ds(pl.multiple_of((s * columns + 2 * target + c) * share, share), share), :]
                for c in (core, 1 - core)
                for s in range(slabs)
            ],
            0,
        )
        for k in range(group):
            held = jnp.zeros(lane.shape, F32)
            for member in range(spread):
                held = held + jnp.where(wanted[:, member : member + 1] == lane + k * tiles, 1.0, 0.0)
            counts[:, k * tiles : (k + 1) * tiles] = held.astype(BF16)
        for z in range(0, slab_rows, 2):
            result = dot(counts[...], table[:, z * tile : (z + 2) * tile])
            result = jnp.floor(result * TURN + 0.5).astype(jnp.int32).astype(I16)
            for more in range(2):
                part = result[:, more * tile : (more + 1) * tile]
                own[d, z + more] = part[: slabs * share].reshape(slabs, share, tile)
                outgoing[d, z + more] = part[slabs * share :].reshape(slabs, share, tile)
        to_pair(d).start()

    def combine(i):
        d, target = at_step(i)
        to_pair(d).wait_recv()

        @pl.loop(0, slab_rows)
        def _(z):
            own[d, z] = own[d, z] + pair[d, z]

        @pl.when(i < 7)
        def _():
            to_chip(d, target).start()

    @pl.loop(0, 9)
    def _(i):
        @pl.when(i < 8)
        def _():
            compute(i)

        @pl.when(i > 0)
        def _():
            combine(i - 1)

    loads[5].wait()
    for slot in range(measured.shape[0]):

        @pl.loop(0, half)
        def _(row):
            both = jnp.concatenate([measured[slot, row], measured[slot, row + half]], 0)
            observed[slot, pl.ds(row, limit, half), :] = both.T

    for i in range(7):
        d, target = at_step(i)
        to_chip(d, target).wait_recv()

    @pl.loop(0, slab_rows)
    def _(z):
        value = own[0, z]
        for d in range(1, 8):
            value = value + arrived[d, z]
        total[:, z] = value

    slabs_ = []
    for d in range(1, 8):
        other = moved(slab, steps_over()[d])
        slabs_.append(
            remote(total.at[other], image.at[slab], slab_send.at[d], slab_recv.at[d], (other, column))
        )
        slabs_[-1].start()
    image[slab] = total[slab]
    for i in range(8):
        d, target = at_step(i)
        to_pair(d).wait_send()
        if i < 7:
            to_chip(d, target).wait_send()
    for copy in slabs_:
        copy.wait()


def forward(volume, templates, pattern, measured, columns, slabs):
    slab_rows, cells = volume.shape
    group, tile_cells, tile = templates.shape
    tiles = cells // tile_cells
    tile_rows, spread, angles = pattern.shape
    slots, size, _, limit = measured.shape
    rows = angles * tile_rows
    share = rows // (columns * slabs)
    block = (columns // 2, slab_rows, slabs, share, tile)
    vector = pl.BlockSpec(memory_space=pltpu.VMEM)
    anywhere = pl.BlockSpec(memory_space=pl.ANY)
    sem = pltpu.SemaphoreType.DMA((8,))
    return pl.pallas_call(
        forward_kernel,
        out_shape=(
            jax.ShapeDtypeStruct((slabs, slab_rows, share, tile), I16),
            jax.ShapeDtypeStruct((slots, limit * size // 2, 2 * size), F32),
        ),
        in_specs=[anywhere, anywhere, vector, anywhere],
        out_specs=(vector, vector),
        scratch_shapes=[
            pltpu.VMEM(volume.shape, BF16),
            pltpu.VMEM(templates.shape, BF16),
            pltpu.VMEM(measured.shape, F32),
            pltpu.VMEM((group, tiles * slab_rows, tile), F32),
            pltpu.VMEM((group * tiles, slab_rows * tile), BF16),
            pltpu.VMEM((2 * slabs * share, group * tiles), BF16),
            pltpu.VMEM((rows, tile), jnp.int32),
        ]
        + [pltpu.VMEM(block, I16)] * 4
        + [pltpu.VMEM((slabs, slab_rows, share, tile), I16)]
        + [sem] * 7,
        compiler_params=pltpu.CompilerParams(
            collective_id=1, has_side_effects=True, vmem_limit_bytes=48 * 2**20
        ),
    )(volume, templates, pattern, measured)


def trig_coefficients():
    grid = (np.cos(np.pi * (np.arange(400) + 0.5) / 400) + 1.0) * (np.pi * np.pi * 0.5005)
    root = np.sqrt(grid)
    sine = np.polynomial.Polynomial.fit(grid, np.sin(root) / root, 6).convert().coef
    cosine = np.polynomial.Polynomial.fit(grid, np.cos(root), 7).convert().coef
    return [float(v) for v in sine], [float(v) for v in cosine]


def sine_cosine(angle):
    sine, cosine = trig_coefficients()
    square = angle * angle
    sine_value = jnp.full_like(square, sine[-1])
    for value in sine[-2::-1]:
        sine_value = sine_value * square + value
    cosine_value = jnp.full_like(square, cosine[-1])
    for value in cosine[-2::-1]:
        cosine_value = cosine_value * square + value
    return sine_value * angle, cosine_value


def split_bf16(table):
    high = table.astype(np.float32).astype(BF16)
    low = (table - high.astype(np.float64)).astype(np.float32).astype(BF16)
    return high, low


def transform_tables(size):
    index = np.arange(size)
    radians = 2.0 * np.pi / size * (index[:, None] * index[None, :] % size)
    cosine = np.cos(radians) / math.sqrt(size)
    sine = np.sin(radians) / math.sqrt(size)
    zero = np.zeros_like(cosine)
    forward = np.block([[cosine, -sine], [sine, cosine]])
    pair = np.block([[cosine, zero, sine, zero], [zero, cosine, zero, sine]])
    back = np.block([[2 * sine, -2 * cosine], [2 * cosine, 2 * sine]])
    f_high, f_low = split_bf16(forward)
    p_high, p_low = split_bf16(pair)
    b_high, b_low = split_bf16(back)
    lanes = np.concatenate([f_high, f_low], 1)
    back = np.concatenate([b_high, b_low], 1)
    return (
        np.concatenate([lanes, lanes], 0),
        np.concatenate([p_high, p_high], 0),
        np.concatenate([p_high, p_low], 0),
        np.concatenate([back, back], 0),
    )


def halves(value):
    high = value.astype(BF16)
    low = (value - high.astype(F32)).astype(BF16)
    return high, low


def ptycho_kernel(
    counts, starts_in, image, probe_wave, t_first, t_pair, t_pair_both, t_back, observed,
    out, waves, total, staged, probe_a, probe_b, starts, landed,
):
    slots = observed.shape[0]
    size = probe_wave.shape[1]
    limit = starts.shape[1]
    owner = lax.axis_index("slab") * lax.axis_size("col") + lax.axis_index("col")
    first_angle = owner * slots
    first_row = lax.div(first_angle, 8) * 8
    load = pltpu.make_async_copy(starts_in.at[pl.ds(pl.multiple_of(first_row, 8), 8)], starts, landed)
    load.start()
    both = jnp.concatenate([probe_wave[0], probe_wave[0]], 0)
    probe_a[...] = both.T
    both = jnp.concatenate([-probe_wave[1], probe_wave[1]], 0)
    probe_b[...] = both.T
    width = waves.shape[0]
    tile = image.shape[1]
    rows = width // tile * slots
    chunk_count = limit // GROUP

    def used_chunks(slot):
        return jnp.clip(lax.div(counts[first_angle + slot] + (GROUP - 1), GROUP), 0, chunk_count)

    half = size // 2

    staged[...] = image[...].astype(jnp.int32).astype(F32) * (2 * math.pi / 65536)
    load.wait()
    lane = lax.broadcasted_iota(jnp.int32, (size, 2 * size), 1)

    @pl.loop(0, slots)
    def _(slot):
        for part in range(width // tile):
            sine, cosine = sine_cosine(staged[pl.ds(slot * (width // tile) + part, size, rows), :])
            waves[part * tile : (part + 1) * tile, :] = jnp.concatenate([cosine, sine], 0).T
        total[...] = jnp.zeros_like(total)
        count = counts[first_angle + slot]

        @pl.loop(0, used_chunks(slot))
        def _(chunk):
            begin = chunk * GROUP
            at = [starts[first_angle - first_row + slot, begin + member] for member in range(GROUP)]
            exits = []
            for member in range(GROUP):
                patch = waves[pl.ds(at[member], size), :]
                exits.append(probe_a[...] * patch + probe_b[...] * pltpu.roll(patch, size, 1))
            exit_wave = jnp.concatenate(exits, 0)
            high, low = halves(exit_wave)
            first = dot(jnp.concatenate([high, low], 1), t_first[...])
            first = first[:, : 2 * size] + first[:, 2 * size :]
            turned = jnp.concatenate(
                [first[pair * 2 * size : (pair + 1) * 2 * size].T for pair in range(GROUP // 2)], 0
            )
            high, low = halves(turned)
            second = dot(jnp.concatenate([high, low], 1), t_pair[...])
            second = second + dot(high, t_pair_both[2 * size :, :])
            scaled = []
            for pair in range(GROUP // 2):
                block = second[pair * 2 * size : (pair + 1) * 2 * size]
                real = block[:size, : 2 * size] + block[size:, 2 * size :]
                imag = block[size:, : 2 * size] - block[:size, 2 * size :]
                member = begin + 2 * pair
                seen = [
                    observed[slot, pl.ds(pl.multiple_of((member + m) * half, half), half), :]
                    for m in range(2)
                ]
                seen = jnp.concatenate(
                    [
                        jnp.concatenate([seen[0][:, :size], seen[1][:, :size]], 1),
                        jnp.concatenate([seen[0][:, size:], seen[1][:, size:]], 1),
                    ],
                    0,
                )
                residual = real * real + imag * imag - seen
                live = member + jnp.where(lane >= size, 1, 0) < count
                residual = jnp.where(live, residual, 0.0)
                scaled += [residual * real, residual * imag]
            scaled = jnp.concatenate(scaled, 0).astype(BF16)
            third = dot(jnp.concatenate([scaled, scaled], 1), t_pair_both[...])
            turned = []
            for pair in range(GROUP // 2):
                block = third[pair * 2 * size : (pair + 1) * 2 * size]
                real = block[:size, : 2 * size] - block[size:, 2 * size :]
                imag = block[size:, : 2 * size] + block[:size, 2 * size :]
                turned.append(jnp.concatenate([real, imag], 0).T)
            high, low = halves(jnp.concatenate(turned, 0))
            back = dot(jnp.concatenate([high, low], 1), t_back[...])
            gradient = exit_wave * (back[:, : 2 * size] + back[:, 2 * size :])
            for member in range(GROUP):
                span = pl.ds(at[member], size)
                total[span, :] = total[span, :] + gradient[member * size : (member + 1) * size]

        for part in range(width // tile):
            flat = total[part * tile : (part + 1) * tile, :].T
            staged[pl.ds(slot * (width // tile) + part, size, rows), :] = flat[:size] + flat[size:]

    out[...] = staged[...].astype(BF16)


def ptycho(image, probe_wave, observed, counts, starts):
    slots = observed.shape[0]
    size = probe_wave.shape[1]
    height, tile = image.shape
    width = height // size // slots * tile
    tables = [jnp.asarray(table) for table in transform_tables(size)]
    vector = pl.BlockSpec(memory_space=pltpu.VMEM)
    return pl.pallas_call(
        ptycho_kernel,
        out_shape=jax.ShapeDtypeStruct((height, tile), BF16),
        in_specs=[pl.BlockSpec(memory_space=pltpu.SMEM), pl.BlockSpec(memory_space=pl.ANY)]
        + [vector] * 7,
        out_specs=vector,
        scratch_shapes=[
            pltpu.VMEM((width, 2 * size), F32),
            pltpu.VMEM((width, 2 * size), F32),
            pltpu.VMEM((height, tile), F32),
            pltpu.VMEM((size, 2 * size), F32),
            pltpu.VMEM((size, 2 * size), F32),
            pltpu.SMEM((8, starts.shape[1]), jnp.int32),
            pltpu.SemaphoreType.DMA,
        ],
        compiler_params=pltpu.CompilerParams(vmem_limit_bytes=48 * 2**20),
    )(counts, starts, image, probe_wave, *tables, observed)


def spread_kernel(
    step_size, penalty,
    gathered, pattern, templates, volume, consensus, out, grads, counts, flat,
):
    columns, slabs, slab_rows, own, tile = gathered.shape
    spread, rows = pattern.shape
    group, tile_cells, _ = templates.shape
    tiles = flat.shape[1] // slab_rows
    here = volume.shape[1] // tile_cells

    @pl.when(pl.program_id(0) == 0)
    def _():
        for z in range(slab_rows):
            grads[:, z * tile : (z + 1) * tile] = gathered[:, :, z].reshape(rows, tile)

        chunk = tiles
        row = lax.broadcasted_iota(jnp.int32, (chunk, 256), 0)

        @pl.loop(0, group)
        def _(k):
            for base in range(0, rows, 256):
                entry = pattern[:, base : base + 256]
                wanted = (entry & (group - 1)) * tiles + lax.shift_right_logical(entry, 3)
                held = jnp.zeros((chunk, 256), F32)
                for member in range(spread):
                    held = held + jnp.where(
                        wanted[member : member + 1, :] == row + k * tiles, 1.0, 0.0
                    )
                counts[pl.ds(pl.multiple_of(k * tiles, tiles), tiles), base : base + 256] = (
                    held.astype(BF16)
                )

        for base in range(0, group, 2):
            for z in range(0, slab_rows, 2):
                result = dot(
                    counts[base * tiles : (base + 2) * tiles, :],
                    grads[:, z * tile : (z + 2) * tile],
                )
                result = result.astype(BF16).astype(F32)
                for k in range(2):
                    for more in range(2):
                        flat[base + k, pl.ds(z + more, tiles, slab_rows), :] = (
                            result[k * tiles : (k + 1) * tiles, more * tile : (more + 1) * tile]
                        )

    size = here * slab_rows
    mine = pl.ds(pl.multiple_of(pl.program_id(0) * size, size), size)
    left = jnp.concatenate([flat[k, mine, :] for k in range(group)], 1).astype(BF16)
    for part in range(0, tile_cells, 256):
        total = jnp.zeros((size, 256), F32)
        for k in range(0, group, 2):
            right = jnp.concatenate(
                [templates[k, part : part + 256, :], templates[k + 1, part : part + 256, :]], 1
            )
            total = total + lax.dot_general(
                left[:, k * tile : (k + 2) * tile],
                right,
                (((1,), (1,)), ((), ())),
                preferred_element_type=F32,
            )
        for t in range(here):
            span = slice(t * tile_cells + part, t * tile_cells + part + 256)
            own_volume = volume[:, span].astype(F32)
            wanted = consensus[:, span].astype(F32)
            moved = total[t * slab_rows : (t + 1) * slab_rows]
            out[:, span] = own_volume - step_size * (moved + penalty * (own_volume - wanted))


def spread_back(gathered, pattern_columns, templates, volume, consensus, step_size, penalty):
    slab_rows, cells = volume.shape
    group, tile_cells, tile = templates.shape
    tiles = cells // tile_cells
    rows = pattern_columns.shape[1]
    vector = pl.BlockSpec(memory_space=pltpu.VMEM)
    steps = 4
    block = pl.BlockSpec((slab_rows, cells // steps), lambda i: (0, i))
    return pl.pallas_call(
        functools.partial(spread_kernel, step_size, penalty),
        grid=(steps,),
        out_shape=jax.ShapeDtypeStruct((slab_rows, cells), F32),
        in_specs=[vector] * 3 + [block, block],
        out_specs=block,
        scratch_shapes=[
            pltpu.VMEM((rows, slab_rows * tile), BF16),
            pltpu.VMEM((group * tiles, rows), BF16),
            pltpu.VMEM((group, tiles * slab_rows, tile), F32),
        ],
        compiler_params=pltpu.CompilerParams(vmem_limit_bytes=48 * 2**20),
    )(gathered, pattern_columns, templates, volume, consensus)


def on_device(
    volume, consensus, templates, pattern, probe_wave, measured, scan_counts, scan_positions
):
    slab_rows = volume.shape[0]
    tile = templates.shape[2]
    slab_count = lax.axis_size("slab")
    column_count = lax.axis_size("col")
    angle_count, tile_rows, spread = pattern.shape[1:]
    per_owner = angle_count // (slab_count * column_count)
    own = per_owner * tile_rows
    rows = angle_count * tile_rows

    image, observed = forward(
        volume,
        templates,
        pattern[0].transpose(1, 2, 0),
        measured.transpose(0, 2, 3, 1),
        column_count,
        slab_count,
    )
    image = image.reshape(slab_count * slab_rows * own, tile)
    gradients = ptycho(image, probe_wave, observed, scan_counts, scan_positions)
    gathered = gather_grads(gradients.reshape(slab_count, slab_rows, own, tile))
    pattern_columns = pattern.reshape(slab_count, column_count, own, spread)
    pattern_columns = pattern_columns.transpose(3, 1, 0, 2).reshape(spread, rows)
    return spread_back(
        gathered, pattern_columns, templates, volume, consensus, step_size, penalty
    )


def solution(mesh):
    return jax.shard_map(
        on_device,
        mesh=mesh,
        in_specs=(
            P("slab", "col"),
            P("slab", "col"),
            P("col", None, None),
            P("col", None, None, None),
            P(),
            P(("slab", "col"), None, None, None),
            P(),
            P(),
        ),
        out_specs=P("slab", "col"),
        check_vma=False,
    )
```

time: 167 us -> 150 us (0.90)
  Pallas kernels: 155 us -> 139 us
    pallas_call x1, Pallas kernels: 31.1 us -> 10.5 us  [ptycho(): pl.pallas_call(ptycho_kernel, out_shape=jax.ShapeDtypeStruct((height, til...]
    pallas_call x1, Pallas kernels: 42.9 us -> 61.9 us  [gather_grads(): pl.pallas_call(gather_kernel, out_shape=jax.ShapeDtypeStruct((16, slabs,...]
    pallas_call x2 -> x1, Pallas kernels: 61.8 us -> 47.4 us  [forward(): pl.pallas_call(forward_kernel, out_shape=(jax.ShapeDtypeStruct((slabs, sl...]
    unnamed x26 -> x27, local copies, waits for them, and re-layouts: 7.85 us -> 7.08 us
where the time goes in v2:
time: 150 us; the launch traced here: 149 us
  Pallas kernels  139 us (93%)
  local copies, waits for them, and re-layouts  9.55 us (6%)
    pallas_call x1, Pallas kernels, gather_grads(): pl.pallas_call(gather_kernel, out_shape=jax.ShapeDtypeStruct((16, slabs,...  61.9 us
    pallas_call x1, Pallas kernels, forward(): pl.pallas_call(forward_kernel, out_shape=(jax.ShapeDtypeStruct((slabs, sl...  47.4 us
    pallas_call x1, Pallas kernels, spread_back(): pl.pallas_call(functools.partial(spread_kernel, step_size, penalty), grid...  19.7 us
    pallas_call x1, Pallas kernels, ptycho(): pl.pallas_call(ptycho_kernel, out_shape=jax.ShapeDtypeStruct((height, til...  10.5 us
    unnamed x27, local copies, waits for them, and re-layouts  7.08 us

profile of v2, /device:TPU:1, one launch (start us, length us, event | category | flops | bytes accessed | tf_op | source)
XLA Modules:
  0.0 149.2 jit_solution(17792141994218841732)
XLA Ops:
  0.0 1.3 copy.13
  1.3 1.0 reshape.14
  2.3 1.2 copy.14
  3.5 0.3 reshape.15.pattern
  3.8 0.0 copy-done.5
  3.8 0.0 copy-done.1
  3.8 0.0 copy-start.2
  3.8 1.6 %copy-done.2 = bf16[8,1024,128]{2,1,0:T(8,128)(2,1)S(1)} copy-done((bf16[8,1024,128]{2,1,0:T(8,128)(2,1)S(1)}, bf16[8,1024,128]{2,1,0:T(8,128)(2,1)}, u32[]{:S(2)}) %copy-start.2) | copy-done | bytes 2097176
  5.4 0.0 copy-start.10
  5.4 0.0 copy-start.11
  5.5 0.0 copy-start.12
  5.5 47.4 %shard_map.118 = (s16[8,8,16,128]{3,2,1,0:T(8,128)(2,1)S(1)}, f32[2,4096,128]{2,1,0:T(8,128)}) custom-call(bf16[8,131072]{1,0:T(8,128)(2,1)S(1)} %copy-done.1, bf16[8,1024,128]{2,1,0:T(8,128)(2,1)S(1)} %copy-done.2, s32[8,8,256]{2,1,0:T(8,128)S(1)} %bitcast.14, f32[2,64,64,128]{3,2,1,0:T(8,128)} %bitcast.16), custom_call_target="tpu_custom_call" | custom-call | tf_op jit(solution)/shard_map/pallas_call | solution.py:295
  52.9 0.0 copy-done.6
  52.9 0.0 copy-done.7
  52.9 0.0 copy-done.8
  52.9 0.0 copy-done.9
  52.9 0.0 copy-done.10
  52.9 0.0 copy-done.11
  53.0 2.2 %copy-done.4 = f32[2,4096,128]{2,1,0:T(8,128)S(1)} copy-done((f32[2,4096,128]{2,1,0:T(8,128)S(1)}, f32[2,4096,128]{2,1,0:T(8,128)}, u32[]{:S(2)}) %copy-start.4) | copy-done | bytes 4194328
  55.1 10.5 %shard_map.119 = bf16[1024,128]{1,0:T(8,128)(2,1)S(1)} custom-call(s32[256]{0:T(256)S(1)} %copy-done.12, s32[256,128]{1,0:T(8,128)S(1)} %copy-done.6, s16[1024,128]{1,0:T(8,128)(2,1)S(1)} %bitcast.15, f32[2,64,64]{2,1,0:T(8,128)S(1)} %copy-done.11, bf16[256,256]{1,0:T(8,128)(2,1)S(1)} %copy-done.10, bf16[256,256]{1,0:T(8,128)(2,1)S(1)} %copy-done.9, ...), custom_call_target="tpu_custom_call" | custom-call | tf_op jit(solution)/shard_map/pallas_call | solution.py:481
  65.7 61.9 %shard_map.120.gathered = bf16[16,8,8,16,128]{4,3,2,1,0:T(8,128)(2,1)S(1)} custom-call(bf16[8,8,16,128]{3,2,1,0:T(8,128)(2,1)S(1)} %bitcast.13), custom_call_target="tpu_custom_call" | custom-call | tf_op jit(solution)/shard_map/pallas_call | solution.py:106
  127.5 1.9 %copy-done = bf16[16,8,8,16,128]{4,3,2,1,0:T(8,128)(2,1)} copy-done((bf16[16,8,8,16,128]{4,3,2,1,0:T(8,128)(2,1)}, bf16[16,8,8,16,128]{4,3,2,1,0:T(8,128)(2,1)S(1)}, u32[]{:S(2)}) %copy-start) | copy-done | bytes 4194328
  129.5 0.0 copy-done.3
  129.5 19.7 %shard_map.121 = f32[8,131072]{1,0:T(8,128)} custom-call(bf16[16,8,8,16,128]{4,3,2,1,0:T(8,128)(2,1)} %copy-done, s32[8,2048]{1,0:T(8,128)S(1)} %reshape.15.pattern, bf16[8,1024,128]{2,1,0:T(8,128)(2,1)S(1)} %copy-done.3, bf16[8,131072]{1,0:T(8,128)(2,1)S(1)} %copy-done.1, bf16[8,131072]{1,0:T(8,128)(2,1)} %consensus.1), custom_call_target="tpu_custom_call" | custom-call | tf_op jit(solution)/shard_map/pallas_call | solution.py:576
  (10 shorter events, 0.0 us)
Async XLA Ops:
  0.0 3.8 %copy-start.5 = (s32[1,256,8,8]{1,3,2,0:T(8,128)S(1)}, s32[1,256,8,8]{1,3,2,0:T(8,128)}, u32[]{:S(2)}) copy-start(s32[1,256,8,8]{1,3,2,0:T(8,128)} %param.15) | copy-start | bytes 196612
  0.0 3.8 %copy-start.1 = (bf16[8,131072]{1,0:T(8,128)(2,1)S(1)}, bf16[8,131072]{1,0:T(8,128)(2,1)}, u32[]{:S(2)}) copy-start(bf16[8,131072]{1,0:T(8,128)(2,1)} %volume.1) | copy-start | bytes 6291460
  3.8 1.6 %copy-start.2 = (bf16[8,1024,128]{2,1,0:T(8,128)(2,1)S(1)}, bf16[8,1024,128]{2,1,0:T(8,128)(2,1)}, u32[]{:S(2)}) copy-start(bf16[8,1024,128]{2,1,0:T(8,128)(2,1)} %templates.1) | copy-start | bytes 6291460
  5.4 47.5 %copy-start.6 = (s32[256,128]{1,0:T(8,128)S(1)}, s32[256,128]{1,0:T(8,128)}, u32[]{:S(2)}) copy-start(s32[256,128]{1,0:T(8,128)} %starts_in.1) | copy-start | bytes 393220
  5.4 47.5 %copy-start.7 = (bf16[256,256]{1,0:T(8,128)(2,1)S(1)}, bf16[256,256]{1,0:T(8,128)(2,1)}, u32[]{:S(2)}) copy-start(bf16[256,256]{1,0:T(8,128)(2,1)} %constant.11.clone.t_back) | copy-start | bytes 393220
  5.4 47.5 %copy-start.8 = (bf16[256,256]{1,0:T(8,128)(2,1)S(1)}, bf16[256,256]{1,0:T(8,128)(2,1)}, u32[]{:S(2)}) copy-start(bf16[256,256]{1,0:T(8,128)(2,1)} %constant.10.clone.t_pair_both) | copy-start | bytes 393220
  5.4 47.5 %copy-start.9 = (bf16[256,256]{1,0:T(8,128)(2,1)S(1)}, bf16[256,256]{1,0:T(8,128)(2,1)}, u32[]{:S(2)}) copy-start(bf16[256,256]{1,0:T(8,128)(2,1)} %constant.9.clone.t_pair) | copy-start | bytes 393220
  5.4 47.5 %copy-start.10 = (bf16[256,256]{1,0:T(8,128)(2,1)S(1)}, bf16[256,256]{1,0:T(8,128)(2,1)}, u32[]{:S(2)}) copy-start(bf16[256,256]{1,0:T(8,128)(2,1)} %constant.8.clone.t_first) | copy-start | bytes 393220
  5.4 47.5 %copy-start.11 = (f32[2,64,64]{2,1,0:T(8,128)S(1)}, f32[2,64,64]{2,1,0:T(8,128)}, u32[]{:S(2)}) copy-start(f32[2,64,64]{2,1,0:T(8,128)} %probe_wave.1) | copy-start | bytes 98308
  5.5 47.5 %copy-start.12 = (s32[256]{0:T(256)S(1)}, s32[256]{0:T(256)}, u32[]{:S(2)}) copy-start(s32[256]{0:T(256)} %counts.1) | copy-start | bytes 3076
  53.0 2.2 %copy-start.4 = (f32[2,4096,128]{2,1,0:T(8,128)S(1)}, f32[2,4096,128]{2,1,0:T(8,128)}, u32[]{:S(2)}) copy-start(f32[2,4096,128]{2,1,0:T(8,128)} %get-tuple-element.8.observed) | copy-start | bytes 12582916
  55.1 74.3 %copy-start.3 = (bf16[8,1024,128]{2,1,0:T(8,128)(2,1)S(1)}, bf16[8,1024,128]{2,1,0:T(8,128)(2,1)}, u32[]{:S(2)}) copy-start(bf16[8,1024,128]{2,1,0:T(8,128)(2,1)} %templates.1) | copy-start | bytes 6291460
  127.5 1.9 %copy-start = (bf16[16,8,8,16,128]{4,3,2,1,0:T(8,128)(2,1)}, bf16[16,8,8,16,128]{4,3,2,1,0:T(8,128)(2,1)S(1)}, u32[]{:S(2)}) copy-start(bf16[16,8,8,16,128]{4,3,2,1,0:T(8,128)(2,1)S(1)} %shard_map.120.gathered) | copy-start | bytes 12582916

commit v3 on v2

--- a/solution.py
+++ b/solution.py
@@ -53,67 +53,6 @@
         device_id=device,
         device_id_type=pl.DeviceIdType.MESH,
     )
-
-
-def gather_kernel(
-    grads, out, mine, held, slab_send, slab_recv, chip_send, chip_recv, pair_send, pair_recv,
-    out_sem,
-):
-    slab, column = lax.axis_index("slab"), lax.axis_index("col")
-    chip, core = lax.div(column, 2), lax.rem(column, 2)
-    sibling = (slab, 2 * chip + 1 - core)
-    steps = steps_over()
-    greet_all(slab, chip, core)
-    greeted(15)
-
-    slabs_, chips, pairs, locals_ = {}, {}, {}, {}
-    for d in range(1, 8):
-        other = moved(slab, steps[d])
-        slabs_[d] = remote(
-            grads.at[other], mine.at[slab], slab_send.at[d], slab_recv.at[d], (other, column)
-        )
-        slabs_[d].start()
-    mine[slab] = grads[slab]
-    for d in range(1, 8):
-        slabs_[d].wait_recv()
-    for d in range(1, 8):
-        target = moved(chip, steps[d])
-        chips[d] = remote(
-            mine, held.at[d], chip_send.at[d], chip_recv.at[d], (slab, 2 * target + core)
-        )
-        chips[d].start()
-    for d in range(8):
-        if d:
-            chips[d].wait_recv()
-        source = mine if d == 0 else held.at[d]
-        origin = moved(chip, ((2 - steps[d][0]) % 2, (4 - steps[d][1]) % 4))
-        place = out.at[2 * origin + core]
-        pairs[d] = remote(source, place, pair_send.at[d], pair_recv.at[d], sibling)
-        pairs[d].start()
-        locals_[d] = pltpu.make_async_copy(source, place, out_sem.at[d])
-        locals_[d].start()
-    for d in range(8):
-        locals_[d].wait()
-        pairs[d].wait()
-        if d:
-            chips[d].wait_send()
-            slabs_[d].wait_send()
-
-
-def gather_grads(grads):
-    slabs, slab_rows, own, tile = grads.shape
-    sem = pltpu.SemaphoreType.DMA((8,))
-    return pl.pallas_call(
-        gather_kernel,
-        out_shape=jax.ShapeDtypeStruct((16, slabs, slab_rows, own, tile), BF16),
-        in_specs=[pl.BlockSpec(memory_space=pltpu.VMEM)],
-        out_specs=pl.BlockSpec(memory_space=pl.ANY),
-        scratch_shapes=[pltpu.VMEM(grads.shape, BF16), pltpu.VMEM((8,) + grads.shape, BF16)]
-        + [sem] * 7,
-        compiler_params=pltpu.CompilerParams(
-            collective_id=2, has_side_effects=True, vmem_limit_bytes=32 * 2**20
-        ),
-    )(grads)
 
 
 def segment_of(entry, group, tiles):
@@ -497,54 +436,153 @@
     )(counts, starts, image, probe_wave, *tables, observed)
 
 
-def spread_kernel(
-    step_size, penalty,
-    gathered, pattern, templates, volume, consensus, out, grads, counts, flat,
+def collect_kernel(
+    grads, pattern, out, mine, held, twin, counts, index, total, flat,
+    slab_send, slab_recv, chip_send, chip_recv, pair_send, pair_recv,
 ):
-    columns, slabs, slab_rows, own, tile = gathered.shape
-    spread, rows = pattern.shape
+    slab, column = lax.axis_index("slab"), lax.axis_index("col")
+    chip, core = lax.div(column, 2), lax.rem(column, 2)
+    sibling = (slab, 2 * chip + 1 - core)
+    steps = steps_over()
+    slabs, slab_rows, share, tile = grads.shape
+    tile_rows, spread, angles = pattern.shape
+    group, _, _ = out.shape
+    tiles = out.shape[1] // slab_rows
+    columns = angles * tile_rows // (slabs * share)
+    greet_all(slab, chip, core)
+    greeted(15)
+
+    order = [1, 3, 4, 2, 5, 7, 6]
+    slabs_, chips, pairs = {}, {}, {}
+    for d in order:
+        other = moved(slab, steps[d])
+        slabs_[d] = remote(
+            grads.at[other], mine.at[slab], slab_send.at[d], slab_recv.at[d], (other, column)
+        )
+        slabs_[d].start()
+    mine[slab] = grads[slab]
+
+    turned = jnp.concatenate(
+        [
+            pattern[:, :, base : base + tile].reshape(-1, tile).T
+            for base in range(0, angles, tile)
+        ],
+        0,
+    )
+    turned = segment_of(turned, group, tiles)
+    for d in range(tile_rows):
+        index[pl.ds(d, angles, tile_rows), :spread] = turned[:, d * spread : (d + 1) * spread]
+
+    for d in order:
+        slabs_[d].wait_recv()
+    for d in order:
+        chips[d] = remote(
+            mine, held.at[d], chip_send.at[d], chip_recv.at[d],
+            (slab, 2 * moved(chip, steps[d]) + core),
+        )
+        chips[d].start()
+    pairs[0] = remote(mine, twin.at[0], pair_send.at[0], pair_recv.at[0], sibling)
+    pairs[0].start()
+
+    row = lax.broadcasted_iota(jnp.int32, (tiles, 2 * slabs * share), 0)
+
+    @pl.loop(0, columns // 2)
+    def _(origin):
+        wanted = jnp.concatenate(
+            [
+                index[pl.ds(pl.multiple_of((s * columns + 2 * origin + c) * share, share), share), :]
+                for c in range(2)
+                for s in range(slabs)
+            ],
+            0,
+        ).T
+        for k in range(group):
+            held_here = jnp.zeros(row.shape, F32)
+            for member in range(spread):
+                held_here = held_here + jnp.where(
+                    wanted[member : member + 1, :] == row + k * tiles, 1.0, 0.0
+                )
+            counts[origin, k * tiles : (k + 1) * tiles, :] = held_here.astype(BF16)
+
+    def add(d, near, far):
+        if d:
+            origin = moved(chip, ((2 - steps[d][0]) % 2, (4 - steps[d][1]) % 4))
+        else:
+            origin = chip
+        swapped = core == 1
+        for z in range(0, slab_rows, 2):
+            parts = []
+            for more in range(2):
+                a = near[:, z + more].reshape(slabs * share, tile)
+                b = far[:, z + more].reshape(slabs * share, tile)
+                parts.append(
+                    jnp.concatenate([jnp.where(swapped, b, a), jnp.where(swapped, a, b)], 0)
+                )
+            right = jnp.concatenate(parts, 1)
+            for base in range(0, group * tiles, 256):
+                result = dot(counts[origin, base : base + 256, :], right)
+                span = slice(base, base + 256)
+                lanes = slice(z * tile, (z + 2) * tile)
+                if d:
+                    result = result + total[span, lanes]
+                total[span, lanes] = result
+
+    pending = 0
+    for d in order + [None]:
+        if d is not None:
+            chips[d].wait_recv()
+            pairs[d] = remote(held.at[d], twin.at[d], pair_send.at[d], pair_recv.at[d], sibling)
+            pairs[d].start()
+        pairs[pending].wait_recv()
+        add(pending, held.at[pending] if pending else mine, twin.at[pending])
+        pending = d
+
+    for k in range(group):
+        for z in range(slab_rows):
+            block = total[k * tiles : (k + 1) * tiles, z * tile : (z + 1) * tile]
+            flat[pl.ds(z, tiles, slab_rows), :] = block
+        out[k] = flat[...].astype(BF16)
+
+    for d in order:
+        slabs_[d].wait_send()
+        chips[d].wait_send()
+    for d in [0] + order:
+        pairs[d].wait_send()
+
+
+def collect(grads, pattern, templates, tiles):
+    slabs, slab_rows, share, tile = grads.shape
     group, tile_cells, _ = templates.shape
-    tiles = flat.shape[1] // slab_rows
-    here = volume.shape[1] // tile_cells
-
-    @pl.when(pl.program_id(0) == 0)
-    def _():
-        for z in range(slab_rows):
-            grads[:, z * tile : (z + 1) * tile] = gathered[:, :, z].reshape(rows, tile)
-
-        chunk = tiles
-        row = lax.broadcasted_iota(jnp.int32, (chunk, 256), 0)
-
-        @pl.loop(0, group)
-        def _(k):
-            for base in range(0, rows, 256):
-                entry = pattern[:, base : base + 256]
-                wanted = (entry & (group - 1)) * tiles + lax.shift_right_logical(entry, 3)
-                held = jnp.zeros((chunk, 256), F32)
-                for member in range(spread):
-                    held = held + jnp.where(
-                        wanted[member : member + 1, :] == row + k * tiles, 1.0, 0.0
-                    )
-                counts[pl.ds(pl.multiple_of(k * tiles, tiles), tiles), base : base + 256] = (
-                    held.astype(BF16)
-                )
-
-        for base in range(0, group, 2):
-            for z in range(0, slab_rows, 2):
-                result = dot(
-                    counts[base * tiles : (base + 2) * tiles, :],
-                    grads[:, z * tile : (z + 2) * tile],
-                )
-                result = result.astype(BF16).astype(F32)
-                for k in range(2):
-                    for more in range(2):
-                        flat[base + k, pl.ds(z + more, tiles, slab_rows), :] = (
-                            result[k * tiles : (k + 1) * tiles, more * tile : (more + 1) * tile]
-                        )
-
-    size = here * slab_rows
-    mine = pl.ds(pl.multiple_of(pl.program_id(0) * size, size), size)
-    left = jnp.concatenate([flat[k, mine, :] for k in range(group)], 1).astype(BF16)
+    tile_rows, spread, angles = pattern.shape
+    columns = angles * tile_rows // (slabs * share)
+    vector = pl.BlockSpec(memory_space=pltpu.VMEM)
+    sem = pltpu.SemaphoreType.DMA((8,))
+    return pl.pallas_call(
+        collect_kernel,
+        out_shape=jax.ShapeDtypeStruct((group, tiles * slab_rows, tile), BF16),
+        in_specs=[vector, vector],
+        out_specs=vector,
+        scratch_shapes=[
+            pltpu.VMEM(grads.shape, BF16),
+            pltpu.VMEM((8,) + grads.shape, BF16),
+            pltpu.VMEM((8,) + grads.shape, BF16),
+            pltpu.VMEM((columns // 2, group * tiles, 2 * slabs * share), BF16),
+            pltpu.VMEM((angles * tile_rows, tile), jnp.int32),
+            pltpu.VMEM((group * tiles, slab_rows * tile), F32),
+            pltpu.VMEM((tiles * slab_rows, tile), F32),
+        ]
+        + [sem] * 6,
+        compiler_params=pltpu.CompilerParams(
+            collective_id=2, has_side_effects=True, vmem_limit_bytes=48 * 2**20
+        ),
+    )(grads, pattern)
+
+
+def update_kernel(sums, templates, volume, consensus, out):
+    group, size, tile = sums.shape
+    tile_cells = templates.shape[1]
+    slab_rows = volume.shape[0]
+    left = jnp.concatenate([sums[k] for k in range(group)], 1)
     for part in range(0, tile_cells, 256):
         total = jnp.zeros((size, 256), F32)
         for k in range(0, group, 2):
@@ -557,35 +595,32 @@
                 (((1,), (1,)), ((), ())),
                 preferred_element_type=F32,
             )
-        for t in range(here):
+        for t in range(size // slab_rows):
             span = slice(t * tile_cells + part, t * tile_cells + part + 256)
             own_volume = volume[:, span].astype(F32)
             wanted = consensus[:, span].astype(F32)
-            moved = total[t * slab_rows : (t + 1) * slab_rows]
-            out[:, span] = own_volume - step_size * (moved + penalty * (own_volume - wanted))
-
-
-def spread_back(gathered, pattern_columns, templates, volume, consensus, step_size, penalty):
+            moved_by = total[t * slab_rows : (t + 1) * slab_rows]
+            out[:, span] = own_volume - step_size * (moved_by + penalty * (own_volume - wanted))
+
+
+def update(sums, templates, volume, consensus):
     slab_rows, cells = volume.shape
-    group, tile_cells, tile = templates.shape
-    tiles = cells // tile_cells
-    rows = pattern_columns.shape[1]
-    vector = pl.BlockSpec(memory_space=pltpu.VMEM)
+    group, height, tile = sums.shape
     steps = 4
     block = pl.BlockSpec((slab_rows, cells // steps), lambda i: (0, i))
     return pl.pallas_call(
-        functools.partial(spread_kernel, step_size, penalty),
+        update_kernel,
         grid=(steps,),
         out_shape=jax.ShapeDtypeStruct((slab_rows, cells), F32),
-        in_specs=[vector] * 3 + [block, block],
+        in_specs=[
+            pl.BlockSpec((group, height // steps, tile), lambda i: (0, i, 0)),
+            pl.BlockSpec(templates.shape, lambda i: (0, 0, 0)),
+            block,
+            block,
+        ],
         out_specs=block,
-        scratch_shapes=[
-            pltpu.VMEM((rows, slab_rows * tile), BF16),
-            pltpu.VMEM((group * tiles, rows), BF16),
-            pltpu.VMEM((group, tiles * slab_rows, tile), F32),
-        ],
         compiler_params=pltpu.CompilerParams(vmem_limit_bytes=48 * 2**20),
-    )(gathered, pattern_columns, templates, volume, consensus)
+    )(sums, templates, volume, consensus)
 
 
 def on_device(
@@ -610,12 +645,13 @@
     )
     image = image.reshape(slab_count * slab_rows * own, tile)
     gradients = ptycho(image, probe_wave, observed, scan_counts, scan_positions)
-    gathered = gather_grads(gradients.reshape(slab_count, slab_rows, own, tile))
-    pattern_columns = pattern.reshape(slab_count, column_count, own, spread)
-    pattern_columns = pattern_columns.transpose(3, 1, 0, 2).reshape(spread, rows)
-    return spread_back(
-        gathered, pattern_columns, templates, volume, consensus, step_size, penalty
+    sums = collect(
+        gradients.reshape(slab_count, slab_rows, own, tile),
+        pattern[0].transpose(1, 2, 0),
+        templates,
+        volume.shape[1] // templates.shape[1],
     )
+    return update(sums, templates, volume, consensus)
 
 
 def solution(mesh):

time: 150 us -> 137 us (0.913)
  Pallas kernels: 139 us -> 130 us
  local copies, waits for them, and re-layouts: 9.55 us -> 6.24 us
    pallas_call x2, Pallas kernels: 81.6 us -> 47.7 us  [the longest x1 41.4 us: collect(): pl.pallas_call(collect_kernel, out_shape=jax.ShapeDtypeStruct((group, til...]
    pallas_call x1, Pallas kernels: 10.5 us -> 35 us  [ptycho(): pl.pallas_call(ptycho_kernel, out_shape=jax.ShapeDtypeStruct((height, til...]
    unnamed x27 -> x26, local copies, waits for them, and re-layouts: 7.08 us -> 6.24 us
where the time goes in v3:
time: 137 us; the launch traced here: 136 us
  Pallas kernels  130 us (95%)
  local copies, waits for them, and re-layouts  6.24 us (5%)
    pallas_call x1, Pallas kernels, forward(): pl.pallas_call(forward_kernel, out_shape=(jax.ShapeDtypeStruct((slabs, sl...  47.4 us
    pallas_call x1, Pallas kernels, collect(): pl.pallas_call(collect_kernel, out_shape=jax.ShapeDtypeStruct((group, til...  41.4 us
    pallas_call x1, Pallas kernels, ptycho(): pl.pallas_call(ptycho_kernel, out_shape=jax.ShapeDtypeStruct((height, til...  35 us
    pallas_call x1, Pallas kernels, update(): pl.pallas_call(update_kernel, grid=(steps,), out_shape=jax.ShapeDtypeStru...  6.3 us
    unnamed x26, local copies, waits for them, and re-layouts  6.24 us

profile of v3, /device:TPU:1, one launch (start us, length us, event | category | flops | bytes accessed | tf_op | source)
XLA Modules:
  0.0 136.4 jit_solution(17111882564337703850)
XLA Ops:
  0.0 0.0 copy-start
  0.0 1.6 %copy-done = bf16[8,131072]{1,0:T(8,128)(2,1)S(1)} copy-done((bf16[8,131072]{1,0:T(8,128)(2,1)S(1)}, bf16[8,131072]{1,0:T(8,128)(2,1)}, u32[]{:S(2)}) %copy-start) | copy-done | bytes 2097176
  1.6 0.0 copy-start.1
  1.6 1.6 %copy-done.1 = bf16[8,1024,128]{2,1,0:T(8,128)(2,1)S(1)} copy-done((bf16[8,1024,128]{2,1,0:T(8,128)(2,1)S(1)}, bf16[8,1024,128]{2,1,0:T(8,128)(2,1)}, u32[]{:S(2)}) %copy-start.1) | copy-done | bytes 2097176
  3.2 0.8 copy-done.4
  4.0 0.0 copy-start.10
  4.0 0.0 copy-start.11
  4.1 0.0 copy-start.12
  4.1 47.4 %shard_map.118 = (s16[8,8,16,128]{3,2,1,0:T(8,128)(2,1)S(1)}, f32[2,4096,128]{2,1,0:T(8,128)}) custom-call(bf16[8,131072]{1,0:T(8,128)(2,1)S(1)} %copy-done, bf16[8,1024,128]{2,1,0:T(8,128)(2,1)S(1)} %copy-done.1, s32[8,8,256]{2,1,0:T(8,128)S(1)} %bitcast.7, f32[2,64,64,128]{3,2,1,0:T(8,128)} %bitcast.10), custom_call_target="tpu_custom_call" | custom-call | tf_op jit(solution)/shard_map/pallas_call | solution.py:234
  51.5 0.0 copy-done.6
  51.5 0.0 copy-done.7
  51.5 0.0 copy-done.8
  51.5 0.0 copy-done.9
  51.5 0.0 copy-done.10
  51.5 0.0 copy-done.11
  51.5 0.0 copy-done.12
  51.5 0.0 copy-start.3
  51.5 2.2 %copy-done.3 = f32[2,4096,128]{2,1,0:T(8,128)S(1)} copy-done((f32[2,4096,128]{2,1,0:T(8,128)S(1)}, f32[2,4096,128]{2,1,0:T(8,128)}, u32[]{:S(2)}) %copy-start.3) | copy-done | bytes 4194328
  53.7 35.0 %shard_map.119 = bf16[1024,128]{1,0:T(8,128)(2,1)S(1)} custom-call(s32[256]{0:T(256)S(1)} %copy-done.12, s32[256,128]{1,0:T(8,128)S(1)} %copy-done.6, s16[1024,128]{1,0:T(8,128)(2,1)S(1)} %bitcast.9, f32[2,64,64]{2,1,0:T(8,128)S(1)} %copy-done.11, bf16[256,256]{1,0:T(8,128)(2,1)S(1)} %copy-done.10, bf16[256,256]{1,0:T(8,128)(2,1)S(1)} %copy-done.9, ...), custom_call_target="tpu_custom_call" | custom-call | tf_op jit(solution)/shard_map/pallas_call | solution.py:420
  88.7 0.0 copy-start.2
  88.8 0.0 copy-done.5
  88.8 41.4 %shard_map.120.sums = bf16[8,1024,128]{2,1,0:T(8,128)(2,1)S(1)} custom-call(bf16[8,8,16,128]{3,2,1,0:T(8,128)(2,1)S(1)} %bitcast.6, s32[8,8,256]{2,1,0:T(8,128)S(1)} %bitcast.8), custom_call_target="tpu_custom_call" | custom-call | tf_op jit(solution)/shard_map/pallas_call | solution.py:560
  130.1 0.0 copy-done.2
  130.1 6.3 %shard_map.121 = f32[8,131072]{1,0:T(8,128)} custom-call(bf16[8,1024,128]{2,1,0:T(8,128)(2,1)S(1)} %shard_map.120.sums, bf16[8,1024,128]{2,1,0:T(8,128)(2,1)S(1)} %copy-done.2, bf16[8,131072]{1,0:T(8,128)(2,1)} %volume.1, bf16[8,131072]{1,0:T(8,128)(2,1)} %consensus.1), custom_call_target="tpu_custom_call" | custom-call | tf_op jit(solution)/shard_map/pallas_call | solution.py:611
  (6 shorter events, 0.0 us)
Async XLA Ops:
  0.0 1.6 %copy-start = (bf16[8,131072]{1,0:T(8,128)(2,1)S(1)}, bf16[8,131072]{1,0:T(8,128)(2,1)}, u32[]{:S(2)}) copy-start(bf16[8,131072]{1,0:T(8,128)(2,1)} %volume.1) | copy-start | bytes 6291460
  1.6 1.6 %copy-start.1 = (bf16[8,1024,128]{2,1,0:T(8,128)(2,1)S(1)}, bf16[8,1024,128]{2,1,0:T(8,128)(2,1)}, u32[]{:S(2)}) copy-start(bf16[8,1024,128]{2,1,0:T(8,128)(2,1)} %templates.1) | copy-start | bytes 6291460
  3.2 0.8 copy-start.4
  4.0 47.4 %copy-start.6 = (s32[256,128]{1,0:T(8,128)S(1)}, s32[256,128]{1,0:T(8,128)}, u32[]{:S(2)}) copy-start(s32[256,128]{1,0:T(8,128)} %starts_in.1) | copy-start | bytes 393220
  4.0 47.5 %copy-start.7 = (bf16[256,256]{1,0:T(8,128)(2,1)S(1)}, bf16[256,256]{1,0:T(8,128)(2,1)}, u32[]{:S(2)}) copy-start(bf16[256,256]{1,0:T(8,128)(2,1)} %constant.11.clone.t_back) | copy-start | bytes 393220
  4.0 47.5 %copy-start.8 = (bf16[256,256]{1,0:T(8,128)(2,1)S(1)}, bf16[256,256]{1,0:T(8,128)(2,1)}, u32[]{:S(2)}) copy-start(bf16[256,256]{1,0:T(8,128)(2,1)} %constant.10.clone.t_pair_both) | copy-start | bytes 393220
  4.0 47.5 %copy-start.9 = (bf16[256,256]{1,0:T(8,128)(2,1)S(1)}, bf16[256,256]{1,0:T(8,128)(2,1)}, u32[]{:S(2)}) copy-start(bf16[256,256]{1,0:T(8,128)(2,1)} %constant.9.clone.t_pair) | copy-start | bytes 393220
  4.0 47.5 %copy-start.10 = (bf16[256,256]{1,0:T(8,128)(2,1)S(1)}, bf16[256,256]{1,0:T(8,128)(2,1)}, u32[]{:S(2)}) copy-start(bf16[256,256]{1,0:T(8,128)(2,1)} %constant.8.clone.t_first) | copy-start | bytes 393220
  4.0 47.5 %copy-start.11 = (f32[2,64,64]{2,1,0:T(8,128)S(1)}, f32[2,64,64]{2,1,0:T(8,128)}, u32[]{:S(2)}) copy-start(f32[2,64,64]{2,1,0:T(8,128)} %probe_wave.1) | copy-start | bytes 98308
  4.1 47.5 %copy-start.12 = (s32[256]{0:T(256)S(1)}, s32[256]{0:T(256)}, u32[]{:S(2)}) copy-start(s32[256]{0:T(256)} %counts.1) | copy-start | bytes 3076
  51.5 2.2 %copy-start.3 = (f32[2,4096,128]{2,1,0:T(8,128)S(1)}, f32[2,4096,128]{2,1,0:T(8,128)}, u32[]{:S(2)}) copy-start(f32[2,4096,128]{2,1,0:T(8,128)} %get-tuple-element.8.observed) | copy-start | bytes 12582916
  53.7 35.0 %copy-start.5 = (s32[1,256,8,8]{1,3,2,0:T(8,128)S(1)}, s32[1,256,8,8]{1,3,2,0:T(8,128)}, u32[]{:S(2)}) copy-start(s32[1,256,8,8]{1,3,2,0:T(8,128)} %param.15) | copy-start | bytes 196612
  88.7 41.4 %copy-start.2 = (bf16[8,1024,128]{2,1,0:T(8,128)(2,1)S(1)}, bf16[8,1024,128]{2,1,0:T(8,128)(2,1)}, u32[]{:S(2)}) copy-start(bf16[8,1024,128]{2,1,0:T(8,128)(2,1)} %templates.1) | copy-start | bytes 6291460

commit v4 on v3

--- a/solution.py
+++ b/solution.py
@@ -11,7 +11,7 @@
 
 BF16 = jnp.bfloat16
 F32 = jnp.float32
-GROUP = 8
+GROUP = 64
 step_size = 0.1
 penalty = 1.0
 I16 = jnp.int16
@@ -61,7 +61,7 @@
 
 def forward_kernel(
     volume_in, templates_in, pattern, measured_in, image, observed,
-    volume, templates, measured, flat, table, counts, index, own, outgoing, pair, arrived, total,
+    volume, templates, measured, turned_over, flat, table, counts, index, own, outgoing, pair, arrived, total,
     load_sem, pair_send, pair_recv, chip_send, chip_recv, slab_send, slab_recv,
 ):
     slab, column = lax.axis_index("slab"), lax.axis_index("col")
@@ -119,7 +119,8 @@
             table[k * tiles : (k + 1) * tiles, z * tile : (z + 1) * tile] = block.astype(BF16)
 
     greeted(15)
-    lane = lax.broadcasted_iota(jnp.int32, (2 * slabs * share, tiles), 1)
+    lane = lax.broadcasted_iota(jnp.int32, (2 * slabs * share, tiles), 1).astype(I16)
+    one, zero = jnp.ones(lane.shape, BF16), jnp.zeros(lane.shape, BF16)
 
     def at_step(i):
         d = lax.rem(5 * i + 5, 8)
@@ -147,11 +148,15 @@
             ],
             0,
         )
+        wide = [
+            jnp.broadcast_to(wanted[:, member : member + 1], lane.shape).astype(I16)
+            for member in range(spread)
+        ]
         for k in range(group):
-            held = jnp.zeros(lane.shape, F32)
+            held = zero
             for member in range(spread):
-                held = held + jnp.where(wanted[:, member : member + 1] == lane + k * tiles, 1.0, 0.0)
-            counts[:, k * tiles : (k + 1) * tiles] = held.astype(BF16)
+                held = held + jnp.where(wide[member] == lane + I16(k * tiles), one, zero)
+            counts[:, k * tiles : (k + 1) * tiles] = held
         for z in range(0, slab_rows, 2):
             result = dot(counts[...], table[:, z * tile : (z + 2) * tile])
             result = jnp.floor(result * TURN + 0.5).astype(jnp.int32).astype(I16)
@@ -184,12 +189,18 @@
             combine(i - 1)
 
     loads[5].wait()
+    stores = []
     for slot in range(measured.shape[0]):
 
         @pl.loop(0, half)
         def _(row):
             both = jnp.concatenate([measured[slot, row], measured[slot, row + half]], 0)
-            observed[slot, pl.ds(row, limit, half), :] = both.T
+            turned_over[slot, pl.ds(row, limit, half), :] = both.T
+
+        stores.append(
+            pltpu.make_async_copy(turned_over.at[slot], observed.at[slot], load_sem.at[6 + slot])
+        )
+        stores[-1].start()
 
     for i in range(7):
         d, target = at_step(i)
@@ -215,7 +226,7 @@
         to_pair(d).wait_send()
         if i < 7:
             to_chip(d, target).wait_send()
-    for copy in slabs_:
+    for copy in slabs_ + stores:
         copy.wait()
 
 
@@ -238,11 +249,12 @@
             jax.ShapeDtypeStruct((slots, limit * size // 2, 2 * size), F32),
         ),
         in_specs=[anywhere, anywhere, vector, anywhere],
-        out_specs=(vector, vector),
+        out_specs=(vector, anywhere),
         scratch_shapes=[
             pltpu.VMEM(volume.shape, BF16),
             pltpu.VMEM(templates.shape, BF16),
             pltpu.VMEM(measured.shape, F32),
+            pltpu.VMEM((slots, limit * size // 2, 2 * size), F32),
             pltpu.VMEM((group, tiles * slab_rows, tile), F32),
             pltpu.VMEM((group * tiles, slab_rows * tile), BF16),
             pltpu.VMEM((2 * slabs * share, group * tiles), BF16),
@@ -252,7 +264,7 @@
         + [pltpu.VMEM((slabs, slab_rows, share, tile), I16)]
         + [sem] * 7,
         compiler_params=pltpu.CompilerParams(
-            collective_id=1, has_side_effects=True, vmem_limit_bytes=48 * 2**20
+            collective_id=1, has_side_effects=True, vmem_limit_bytes=56 * 2**20
         ),
     )(volume, templates, pattern, measured)
 
@@ -312,8 +324,8 @@
 
 
 def ptycho_kernel(
-    counts, starts_in, image, probe_wave, t_first, t_pair, t_pair_both, t_back, observed,
-    out, waves, total, staged, probe_a, probe_b, starts, landed,
+    counts, starts_in, image, probe_wave, t_first, t_pair, t_pair_both, t_back, observed_in,
+    out, waves, total, staged, probe_a, probe_b, observed, starts, landed, here,
 ):
     slots = observed.shape[0]
     size = probe_wave.shape[1]
@@ -323,6 +335,12 @@
     first_row = lax.div(first_angle, 8) * 8
     load = pltpu.make_async_copy(starts_in.at[pl.ds(pl.multiple_of(first_row, 8), 8)], starts, landed)
     load.start()
+    fetches = [
+        pltpu.make_async_copy(observed_in.at[slot], observed.at[slot], here.at[slot])
+        for slot in range(slots)
+    ]
+    for fetch in fetches:
+        fetch.start()
     both = jnp.concatenate([probe_wave[0], probe_wave[0]], 0)
     probe_a[...] = both.T
     both = jnp.concatenate([-probe_wave[1], probe_wave[1]], 0)
@@ -343,6 +361,7 @@
 
     @pl.loop(0, slots)
     def _(slot):
+        pltpu.make_async_copy(observed_in.at[slot], observed.at[slot], here.at[slot]).wait()
         for part in range(width // tile):
             sine, cosine = sine_cosine(staged[pl.ds(slot * (width // tile) + part, size, rows), :])
             waves[part * tile : (part + 1) * tile, :] = jnp.concatenate([cosine, sine], 0).T
@@ -421,7 +440,8 @@
         ptycho_kernel,
         out_shape=jax.ShapeDtypeStruct((height, tile), BF16),
         in_specs=[pl.BlockSpec(memory_space=pltpu.SMEM), pl.BlockSpec(memory_space=pl.ANY)]
-        + [vector] * 7,
+        + [vector] * 6
+        + [pl.BlockSpec(memory_space=pl.ANY)],
         out_specs=vector,
         scratch_shapes=[
             pltpu.VMEM((width, 2 * size), F32),
@@ -429,10 +449,12 @@
             pltpu.VMEM((height, tile), F32),
             pltpu.VMEM((size, 2 * size), F32),
             pltpu.VMEM((size, 2 * size), F32),
+            pltpu.VMEM(observed.shape, F32),
             pltpu.SMEM((8, starts.shape[1]), jnp.int32),
             pltpu.SemaphoreType.DMA,
+            pltpu.SemaphoreType.DMA((slots,)),
         ],
-        compiler_params=pltpu.CompilerParams(vmem_limit_bytes=48 * 2**20),
+        compiler_params=pltpu.CompilerParams(vmem_limit_bytes=56 * 2**20),
     )(counts, starts, image, probe_wave, *tables, observed)
 
 
@@ -484,7 +506,8 @@
     pairs[0] = remote(mine, twin.at[0], pair_send.at[0], pair_recv.at[0], sibling)
     pairs[0].start()
 
-    row = lax.broadcasted_iota(jnp.int32, (tiles, 2 * slabs * share), 0)
+    row = lax.broadcasted_iota(jnp.int32, (tiles, 2 * slabs * share), 0).astype(I16)
+    one, zero = jnp.ones(row.shape, BF16), jnp.zeros(row.shape, BF16)
 
     @pl.loop(0, columns // 2)
     def _(origin):
@@ -496,13 +519,15 @@
             ],
             0,
         ).T
+        wide = [
+            jnp.broadcast_to(wanted[member : member + 1, :], row.shape).astype(I16)
+            for member in range(spread)
+        ]
         for k in range(group):
-            held_here = jnp.zeros(row.shape, F32)
+            held_here = zero
             for member in range(spread):
-                held_here = held_here + jnp.where(
-                    wanted[member : member + 1, :] == row + k * tiles, 1.0, 0.0
-                )
-            counts[origin, k * tiles : (k + 1) * tiles, :] = held_here.astype(BF16)
+                held_here = held_here + jnp.where(wide[member] == row + I16(k * tiles), one, zero)
+            counts[origin, k * tiles : (k + 1) * tiles, :] = held_here
 
     def add(d, near, far):
         if d:
@@ -573,7 +598,7 @@
         ]
         + [sem] * 6,
         compiler_params=pltpu.CompilerParams(
-            collective_id=2, has_side_effects=True, vmem_limit_bytes=48 * 2**20
+            collective_id=2, has_side_effects=True, vmem_limit_bytes=56 * 2**20
         ),
     )(grads, pattern)
 
@@ -619,7 +644,7 @@
             block,
         ],
         out_specs=block,
-        compiler_params=pltpu.CompilerParams(vmem_limit_bytes=48 * 2**20),
+        compiler_params=pltpu.CompilerParams(vmem_limit_bytes=56 * 2**20),
     )(sums, templates, volume, consensus)
 
 

time: 137 us -> 120 us (0.88)
  Pallas kernels: 130 us -> 120 us
  local copies, waits for them, and re-layouts: 6.24 us -> 0 us
    pallas_call x1, Pallas kernels: 35 us -> 20.2 us  [ptycho(): pl.pallas_call(ptycho_kernel, out_shape=jax.ShapeDtypeStruct((height, til...]
    unnamed x26 -> x0, local copies, waits for them, and re-layouts: 6.24 us -> none
    pallas_call x1, Pallas kernels: 41.4 us -> 44.6 us  [collect(): pl.pallas_call(collect_kernel, out_shape=jax.ShapeDtypeStruct((group, til...]
where the time goes in v4:
time: 120 us
  Pallas kernels  120 us (100%)
    pallas_call x1, Pallas kernels, forward(): pl.pallas_call(forward_kernel, out_shape=(jax.ShapeDtypeStruct((slabs, sl...  47.5 us
    pallas_call x1, Pallas kernels, collect(): pl.pallas_call(collect_kernel, out_shape=jax.ShapeDtypeStruct((group, til...  44.6 us
    pallas_call x1, Pallas kernels, ptycho(): pl.pallas_call(ptycho_kernel, out_shape=jax.ShapeDtypeStruct((height, til...  20.2 us
    pallas_call x1, Pallas kernels, update(): pl.pallas_call(update_kernel, grid=(steps,), out_shape=jax.ShapeDtypeStru...  7.38 us

profile of v4, /device:TPU:1, one launch (start us, length us, event | category | flops | bytes accessed | tf_op | source)
XLA Modules:
  0.0 119.7 jit_solution(1325645128388293230)
XLA Ops:
  0.0 47.5 %shard_map.118 = (s16[8,8,16,128]{3,2,1,0:T(8,128)(2,1)}, f32[2,4096,128]{2,1,0:T(8,128)}) custom-call(bf16[8,131072]{1,0:T(8,128)(2,1)} %volume.1, bf16[8,1024,128]{2,1,0:T(8,128)(2,1)} %templates.1, s32[8,8,256]{2,1,0:T(8,128)} %bitcast.8, f32[2,64,64,128]{3,2,1,0:T(8,128)} %bitcast.6), custom_call_target="tpu_custom_call" | custom-call | tf_op jit(solution)/shard_map/pallas_call | solution.py:245
  47.5 20.2 %shard_map.119 = bf16[1024,128]{1,0:T(8,128)(2,1)} custom-call(s32[256]{0:T(256)} %counts.1, s32[256,128]{1,0:T(8,128)} %starts_in.1, s16[1024,128]{1,0:T(8,128)(2,1)} %bitcast.10, f32[2,64,64]{2,1,0:T(8,128)} %probe_wave.1, bf16[256,256]{1,0:T(8,128)(2,1)} %constant.8.clone.t_first, bf16[256,256]{1,0:T(8,128)(2,1)} %constant.9.clone.t_pair, ...), custom_call_target="tpu_custom_call" | custom-call | tf_op jit(solution)/shard_map/pallas_call | solution.py:439
  67.6 44.6 %shard_map.120.sums = bf16[8,1024,128]{2,1,0:T(8,128)(2,1)} custom-call(bf16[8,8,16,128]{3,2,1,0:T(8,128)(2,1)} %bitcast.7, s32[8,8,256]{2,1,0:T(8,128)} %bitcast.9), custom_call_target="tpu_custom_call" | custom-call | tf_op jit(solution)/shard_map/pallas_call | solution.py:585
  112.3 7.4 %shard_map.121 = f32[8,131072]{1,0:T(8,128)} custom-call(bf16[8,1024,128]{2,1,0:T(8,128)(2,1)} %shard_map.120.sums, bf16[8,1024,128]{2,1,0:T(8,128)(2,1)} %templates.1, bf16[8,131072]{1,0:T(8,128)(2,1)} %volume.1, bf16[8,131072]{1,0:T(8,128)(2,1)} %consensus.1), custom_call_target="tpu_custom_call" | custom-call | tf_op jit(solution)/shard_map/pallas_call | solution.py:636

commit v5 on v4

--- a/solution.py
+++ b/solution.py
@@ -30,12 +30,12 @@
     return lax.rem(high + step[0], 2) * 4 + lax.rem(low + step[1], 4)
 
 
-def greet_all(slab, chip, core):
+def greet_near(slab, chip, core):
     barrier = pltpu.get_barrier_semaphore()
-    here = slab, 2 * chip + core
+    column = 2 * chip + core
     others = [(slab, 2 * chip + 1 - core)]
-    others += [(slab, 2 * moved(chip, step) + core) for step in steps_over()[1:]]
-    others += [(moved(slab, step), here[1]) for step in steps_over()[1:]]
+    others += [(slab, 2 * moved(chip, step) + core) for step in steps_over()[1:5]]
+    others += [(moved(slab, step), column) for step in steps_over()[1:]]
     for other in others:
         pl.semaphore_signal(barrier, inc=1, device_id=other, device_id_type=pl.DeviceIdType.MESH)
 
@@ -61,8 +61,8 @@
 
 def forward_kernel(
     volume_in, templates_in, pattern, measured_in, image, observed,
-    volume, templates, measured, turned_over, flat, table, counts, index, own, outgoing, pair, arrived, total,
-    load_sem, pair_send, pair_recv, chip_send, chip_recv, slab_send, slab_recv,
+    volume, templates, measured, turned_over, flat, table, counts, index, own, outgoing, pair, from_y, from_x, total,
+    load_sem, pair_send, pair_recv, x_send, x_recv, y_send, y_recv, slab_send, slab_recv,
 ):
     slab, column = lax.axis_index("slab"), lax.axis_index("col")
     chip, core = lax.div(column, 2), lax.rem(column, 2)
@@ -74,7 +74,7 @@
     half = measured.shape[1] // 2
     limit = measured.shape[3]
     quarter = volume.shape[1] // 4
-    greet_all(slab, chip, core)
+    greet_near(slab, chip, core)
 
     loads = [pltpu.make_async_copy(templates_in, templates, load_sem.at[0])]
     for part in range(4):
@@ -118,14 +118,21 @@
             block = flat[k, pl.ds(z, tiles, slab_rows), :]
             table[k * tiles : (k + 1) * tiles, z * tile : (z + 1) * tile] = block.astype(BF16)
 
-    greeted(15)
+    greeted(12)
     lane = lax.broadcasted_iota(jnp.int32, (2 * slabs * share, tiles), 1).astype(I16)
     one, zero = jnp.ones(lane.shape, BF16), jnp.zeros(lane.shape, BF16)
 
+    low, high = slice(0, slab_rows // 2), slice(slab_rows // 2, slab_rows)
+    across = (slab, 2 * moved(chip, (1, 0)) + core)
+
     def at_step(i):
-        d = lax.rem(5 * i + 5, 8)
-        high = lax.rem(lax.div(chip, 4) + lax.div(d, 4), 2)
-        return d, 4 * high + lax.rem(chip + d, 4)
+        dy = lax.rem(i + 1, 4)
+        far = 1 - lax.div(i, 4)
+        ahead = lax.rem(lax.div(chip, 4) + far, 2)
+        return 4 * far + dy, dy, 4 * ahead + lax.rem(chip + dy, 4)
+
+    def along(dy):
+        return (slab, 2 * (4 * lax.div(chip, 4) + lax.rem(chip + dy, 4)) + core)
 
     def to_pair(d):
         return remote(
@@ -133,13 +140,24 @@
             (slab, 2 * chip + 1 - core),
         )
 
-    def to_chip(d, target):
+    def low_across(dy):
         return remote(
-            own.at[d], arrived.at[d], chip_send.at[d], chip_recv.at[d], (slab, 2 * target + core)
-        )
+            own.at[4 + dy, low], from_x.at[dy, low], x_send.at[dy], x_recv.at[dy], across
+        )
+
+    def low_along(dy):
+        return remote(own.at[dy, low], from_y.at[dy, low], y_send.at[dy], y_recv.at[dy], along(dy))
+
+    def high_along(d, dy):
+        return remote(
+            own.at[d, high], from_y.at[d, high], y_send.at[8 + d], y_recv.at[8 + d], along(dy)
+        )
+
+    def high_across():
+        return remote(own.at[4, high], from_x.at[0, high], x_send.at[4], x_recv.at[4], across)
 
     def compute(i):
-        d, target = at_step(i)
+        d, _, target = at_step(i)
         wanted = jnp.concatenate(
             [
                 index[pl.ds(pl.multiple_of((s * columns + 2 * target + c) * share, share), share), :]
@@ -167,16 +185,32 @@
         to_pair(d).start()
 
     def combine(i):
-        d, target = at_step(i)
+        d, dy, _ = at_step(i)
         to_pair(d).wait_recv()
 
         @pl.loop(0, slab_rows)
         def _(z):
             own[d, z] = own[d, z] + pair[d, z]
 
-        @pl.when(i < 7)
+        @pl.when(lax.rem(i, 4) < 3)
         def _():
-            to_chip(d, target).start()
+            high_along(d, dy).start()
+
+        @pl.when(i < 4)
+        def _():
+            low_across(dy).start()
+
+        @pl.when(i > 3)
+        def _():
+            low_across(dy).wait_recv()
+
+            @pl.loop(0, slab_rows // 2)
+            def _(z):
+                own[dy, z] = own[dy, z] + from_x[dy, z]
+
+        @pl.when((i > 3) & (i < 7))
+        def _():
+            low_along(dy).start()
 
     @pl.loop(0, 9)
     def _(i):
@@ -188,6 +222,18 @@
         def _():
             combine(i - 1)
 
+    for dy in range(1, 4):
+        high_along(4 + dy, dy).wait_recv()
+
+    @pl.loop(slab_rows // 2, slab_rows)
+    def _(z):
+        value = own[4, z]
+        for dy in range(1, 4):
+            value = value + from_y[4 + dy, z]
+        own[4, z] = value
+
+    high_across().start()
+
     loads[5].wait()
     stores = []
     for slot in range(measured.shape[0]):
@@ -202,31 +248,50 @@
         )
         stores[-1].start()
 
-    for i in range(7):
-        d, target = at_step(i)
-        to_chip(d, target).wait_recv()
-
-    @pl.loop(0, slab_rows)
-    def _(z):
-        value = own[0, z]
+    def to_slab(d, part):
+        other = moved(slab, steps_over()[d])
+        side = (low, high)[part]
+        number = 8 * part + d
+        return remote(
+            total.at[other, side], image.at[slab, side], slab_send.at[number], slab_recv.at[number],
+            (other, column),
+        )
+
+    for part in range(2):
+        for dy in range(1, 4):
+            if part:
+                high_along(dy, dy).wait_recv()
+            else:
+                low_along(dy).wait_recv()
+        if part:
+            high_across().wait_recv()
+
+        @pl.loop(part * slab_rows // 2, (part + 1) * slab_rows // 2)
+        def _(z):
+            value = own[0, z]
+            for dy in range(1, 4):
+                value = value + from_y[dy, z]
+            if part:
+                value = value + from_x[0, z]
+            total[:, z] = value
+
         for d in range(1, 8):
-            value = value + arrived[d, z]
-        total[:, z] = value
-
-    slabs_ = []
-    for d in range(1, 8):
-        other = moved(slab, steps_over()[d])
-        slabs_.append(
-            remote(total.at[other], image.at[slab], slab_send.at[d], slab_recv.at[d], (other, column))
-        )
-        slabs_[-1].start()
+            to_slab(d, part).start()
+
     image[slab] = total[slab]
-    for i in range(8):
-        d, target = at_step(i)
+    for d in range(8):
         to_pair(d).wait_send()
-        if i < 7:
-            to_chip(d, target).wait_send()
-    for copy in slabs_ + stores:
+    for dy in range(4):
+        low_across(dy).wait_send()
+        if dy:
+            low_along(dy).wait_send()
+            high_along(dy, dy).wait_send()
+            high_along(4 + dy, dy).wait_send()
+    high_across().wait_send()
+    for part in range(2):
+        for d in range(1, 8):
+            to_slab(d, part).wait()
+    for copy in stores:
         copy.wait()
 
 
@@ -261,8 +326,10 @@
             pltpu.VMEM((rows, tile), jnp.int32),
         ]
         + [pltpu.VMEM(block, I16)] * 4
+        + [pltpu.VMEM((4,) + block[1:], I16)]
         + [pltpu.VMEM((slabs, slab_rows, share, tile), I16)]
-        + [sem] * 7,
+        + [sem] * 5
+        + [pltpu.SemaphoreType.DMA((16,))] * 4,
         compiler_params=pltpu.CompilerParams(
             collective_id=1, has_side_effects=True, vmem_limit_bytes=56 * 2**20
         ),
@@ -461,6 +528,7 @@
 def collect_kernel(
     grads, pattern, out, mine, held, twin, counts, index, total, flat,
     slab_send, slab_recv, chip_send, chip_recv, pair_send, pair_recv,
+    low_send, low_recv, high_send, high_recv,
 ):
     slab, column = lax.axis_index("slab"), lax.axis_index("col")
     chip, core = lax.div(column, 2), lax.rem(column, 2)
@@ -471,8 +539,8 @@
     group, _, _ = out.shape
     tiles = out.shape[1] // slab_rows
     columns = angles * tile_rows // (slabs * share)
-    greet_all(slab, chip, core)
-    greeted(15)
+    greet_near(slab, chip, core)
+    greeted(12)
 
     order = [1, 3, 4, 2, 5, 7, 6]
     slabs_, chips, pairs = {}, {}, {}
@@ -497,12 +565,23 @@
 
     for d in order:
         slabs_[d].wait_recv()
-    for d in order:
+    low, high = slice(0, slab_rows // 2), slice(slab_rows // 2, slab_rows)
+    across = (slab, 2 * moved(chip, (1, 0)) + core)
+    along = {dy: (slab, 2 * moved(chip, (0, dy)) + core) for dy in range(1, 4)}
+    for d in order[:4]:
         chips[d] = remote(
-            mine, held.at[d], chip_send.at[d], chip_recv.at[d],
-            (slab, 2 * moved(chip, steps[d]) + core),
+            mine, held.at[d], chip_send.at[d], chip_recv.at[d], across if d == 4 else along[d]
         )
         chips[d].start()
+    lows, highs = {}, {}
+    for dy in range(1, 4):
+        lows[dy] = remote(
+            held.at[dy, :, low], held.at[4 + dy, :, low], low_send.at[dy], low_recv.at[dy], across
+        )
+        highs[dy] = remote(
+            held.at[4, :, high], held.at[4 + dy, :, high], high_send.at[dy], high_recv.at[dy],
+            along[dy],
+        )
     pairs[0] = remote(mine, twin.at[0], pair_send.at[0], pair_recv.at[0], sibling)
     pairs[0].start()
 
@@ -555,7 +634,16 @@
     pending = 0
     for d in order + [None]:
         if d is not None:
-            chips[d].wait_recv()
+            if d < 5:
+                chips[d].wait_recv()
+            else:
+                lows[d - 4].wait_recv()
+                highs[d - 4].wait_recv()
+            if d < 4:
+                lows[d].start()
+            elif d == 4:
+                for dy in range(1, 4):
+                    highs[dy].start()
             pairs[d] = remote(held.at[d], twin.at[d], pair_send.at[d], pair_recv.at[d], sibling)
             pairs[d].start()
         pairs[pending].wait_recv()
@@ -570,7 +658,11 @@
 
     for d in order:
         slabs_[d].wait_send()
+    for d in order[:4]:
         chips[d].wait_send()
+    for dy in range(1, 4):
+        lows[dy].wait_send()
+        highs[dy].wait_send()
     for d in [0] + order:
         pairs[d].wait_send()
 
@@ -596,7 +688,7 @@
             pltpu.VMEM((group * tiles, slab_rows * tile), F32),
             pltpu.VMEM((tiles * slab_rows, tile), F32),
         ]
-        + [sem] * 6,
+        + [sem] * 10,
         compiler_params=pltpu.CompilerParams(
             collective_id=2, has_side_effects=True, vmem_limit_bytes=56 * 2**20
         ),

time: 120 us -> 107 us (0.89); the launches traced: 120 us -> 105 us
  Pallas kernels: 120 us -> 105 us
    pallas_call x1, Pallas kernels: 20.2 us -> 12.4 us  [ptycho(): pl.pallas_call(ptycho_kernel, out_shape=jax.ShapeDtypeStruct((height, til...]
    pallas_call x1, Pallas kernels: 47.5 us -> 41.8 us  [forward(): pl.pallas_call(forward_kernel, out_shape=(jax.ShapeDtypeStruct((slabs, sl...]
where the time goes in v5:
time: 107 us; the launch traced here: 105 us
  Pallas kernels  105 us (98%)
    pallas_call x1, Pallas kernels, collect(): pl.pallas_call(collect_kernel, out_shape=jax.ShapeDtypeStruct((group, til...  43.6 us
    pallas_call x1, Pallas kernels, forward(): pl.pallas_call(forward_kernel, out_shape=(jax.ShapeDtypeStruct((slabs, sl...  41.8 us
    pallas_call x1, Pallas kernels, ptycho(): pl.pallas_call(ptycho_kernel, out_shape=jax.ShapeDtypeStruct((height, til...  12.4 us
    pallas_call x1, Pallas kernels, update(): pl.pallas_call(update_kernel, grid=(steps,), out_shape=jax.ShapeDtypeStru...  7.38 us

profile of v5, /device:TPU:1, one launch (start us, length us, event | category | flops | bytes accessed | tf_op | source)
XLA Modules:
  0.0 105.3 jit_solution(11721498471090184141)
XLA Ops:
  0.0 41.8 %shard_map.118 = (s16[8,8,16,128]{3,2,1,0:T(8,128)(2,1)}, f32[2,4096,128]{2,1,0:T(8,128)}) custom-call(bf16[8,131072]{1,0:T(8,128)(2,1)} %volume.1, bf16[8,1024,128]{2,1,0:T(8,128)(2,1)} %templates.1, s32[8,8,256]{2,1,0:T(8,128)} %bitcast.8, f32[2,64,64,128]{3,2,1,0:T(8,128)} %bitcast.6), custom_call_target="tpu_custom_call" | custom-call | tf_op jit(solution)/shard_map/pallas_call | solution.py:310
  41.9 12.4 %shard_map.119 = bf16[1024,128]{1,0:T(8,128)(2,1)} custom-call(s32[256]{0:T(256)} %counts.1, s32[256,128]{1,0:T(8,128)} %starts_in.1, s16[1024,128]{1,0:T(8,128)(2,1)} %bitcast.10, f32[2,64,64]{2,1,0:T(8,128)} %probe_wave.1, bf16[256,256]{1,0:T(8,128)(2,1)} %constant.8.clone.t_first, bf16[256,256]{1,0:T(8,128)(2,1)} %constant.9.clone.t_pair, ...), custom_call_target="tpu_custom_call" | custom-call | tf_op jit(solution)/shard_map/pallas_call | solution.py:506
  54.3 43.6 %shard_map.120.sums = bf16[8,1024,128]{2,1,0:T(8,128)(2,1)} custom-call(bf16[8,8,16,128]{3,2,1,0:T(8,128)(2,1)} %bitcast.7, s32[8,8,256]{2,1,0:T(8,128)} %bitcast.9), custom_call_target="tpu_custom_call" | custom-call | tf_op jit(solution)/shard_map/pallas_call | solution.py:677
  97.9 7.4 %shard_map.121 = f32[8,131072]{1,0:T(8,128)} custom-call(bf16[8,1024,128]{2,1,0:T(8,128)(2,1)} %shard_map.120.sums, bf16[8,1024,128]{2,1,0:T(8,128)(2,1)} %templates.1, bf16[8,131072]{1,0:T(8,128)(2,1)} %volume.1, bf16[8,131072]{1,0:T(8,128)(2,1)} %consensus.1), custom_call_target="tpu_custom_call" | custom-call | tf_op jit(solution)/shard_map/pallas_call | solution.py:728

commit v6 on v5

--- a/solution.py
+++ b/solution.py
@@ -34,7 +34,7 @@
     barrier = pltpu.get_barrier_semaphore()
     column = 2 * chip + core
     others = [(slab, 2 * chip + 1 - core)]
-    others += [(slab, 2 * moved(chip, step) + core) for step in steps_over()[1:5]]
+    others += [(slab, 2 * moved(chip, step) + core) for step in ((0, 1), (0, 3), (1, 0))]
     others += [(moved(slab, step), column) for step in steps_over()[1:]]
     for other in others:
         pl.semaphore_signal(barrier, inc=1, device_id=other, device_id_type=pl.DeviceIdType.MESH)
@@ -118,18 +118,13 @@
             block = flat[k, pl.ds(z, tiles, slab_rows), :]
             table[k * tiles : (k + 1) * tiles, z * tile : (z + 1) * tile] = block.astype(BF16)
 
-    greeted(12)
+    greeted(11)
     lane = lax.broadcasted_iota(jnp.int32, (2 * slabs * share, tiles), 1).astype(I16)
     one, zero = jnp.ones(lane.shape, BF16), jnp.zeros(lane.shape, BF16)
 
+    quarter_rows = slab_rows // 4
     low, high = slice(0, slab_rows // 2), slice(slab_rows // 2, slab_rows)
     across = (slab, 2 * moved(chip, (1, 0)) + core)
-
-    def at_step(i):
-        dy = lax.rem(i + 1, 4)
-        far = 1 - lax.div(i, 4)
-        ahead = lax.rem(lax.div(chip, 4) + far, 2)
-        return 4 * far + dy, dy, 4 * ahead + lax.rem(chip + dy, 4)
 
     def along(dy):
         return (slab, 2 * (4 * lax.div(chip, 4) + lax.rem(chip + dy, 4)) + core)
@@ -153,11 +148,29 @@
             own.at[d, high], from_y.at[d, high], y_send.at[8 + d], y_recv.at[8 + d], along(dy)
         )
 
+    def relay(d, side, dy):
+        begin = side * (slab_rows // 2) + (dy // 2) * quarter_rows
+        rows = slice(begin, begin + quarter_rows)
+        number = 16 + 4 * lax.div(d, 4) + 2 * side + dy // 2
+        return remote(
+            own.at[d, rows], from_y.at[d, rows], y_send.at[number], y_recv.at[number], along(dy)
+        )
+
+    def take(d, side, dy):
+        middle = d - dy + 2
+        relay(middle, side, dy).wait_recv()
+        begin = side * (slab_rows // 2) + (dy // 2) * quarter_rows
+
+        @pl.loop(begin, begin + quarter_rows)
+        def _(z):
+            own[d, z] = own[d, z] + from_y[middle, z]
+
     def high_across():
         return remote(own.at[4, high], from_x.at[0, high], x_send.at[4], x_recv.at[4], across)
 
-    def compute(i):
-        d, _, target = at_step(i)
+    def compute(d):
+        ahead = lax.rem(lax.div(chip, 4) + lax.div(d, 4), 2)
+        target = 4 * ahead + lax.rem(chip + d, 4)
         wanted = jnp.concatenate(
             [
                 index[pl.ds(pl.multiple_of((s * columns + 2 * target + c) * share, share), share), :]
@@ -184,61 +197,88 @@
                 outgoing[d, z + more] = part[slabs * share :].reshape(slabs, share, tile)
         to_pair(d).start()
 
-    def combine(i):
-        d, dy, _ = at_step(i)
+    def add_pair(d):
         to_pair(d).wait_recv()
 
         @pl.loop(0, slab_rows)
         def _(z):
             own[d, z] = own[d, z] + pair[d, z]
 
-        @pl.when(lax.rem(i, 4) < 3)
-        def _():
-            high_along(d, dy).start()
-
-        @pl.when(i < 4)
-        def _():
-            low_across(dy).start()
-
-        @pl.when(i > 3)
-        def _():
-            low_across(dy).wait_recv()
-
-            @pl.loop(0, slab_rows // 2)
-            def _(z):
-                own[dy, z] = own[dy, z] + from_x[dy, z]
-
-        @pl.when((i > 3) & (i < 7))
-        def _():
-            low_along(dy).start()
-
-    @pl.loop(0, 9)
-    def _(i):
+    def add_low(dy):
+        low_across(dy).wait_recv()
+
+        @pl.loop(0, slab_rows // 2)
+        def _(z):
+            own[dy, z] = own[dy, z] + from_x[dy, z]
+
+    def send_relays(d, side):
+        for way in (1, 3):
+            relay(d, side, way).start()
+
+    def finish_high(d, way):
+        take(d, 1, way)
+        high_along(d, way).start()
+
+    def finish_low(way):
+        add_low(way)
+        take(way, 0, way)
+        low_along(way).start()
+
+    def turn_corner():
+        for dy in (1, 3):
+            high_along(4 + dy, dy).wait_recv()
+
+        @pl.loop(slab_rows // 2, slab_rows)
+        def _(z):
+            own[4, z] = own[4, z] + from_y[5, z] + from_y[7, z]
+
+        high_across().start()
+
+    plan = {
+        1: [lambda: low_across(2).start(), lambda: send_relays(6, 1)],
+        2: [lambda: send_relays(2, 1)],
+        3: [lambda: low_across(1).start(), lambda: finish_high(5, 1)],
+        4: [
+            lambda: low_across(3).start(),
+            lambda: finish_high(7, 3),
+            lambda: add_low(2),
+            lambda: send_relays(2, 0),
+        ],
+        5: [lambda: low_across(0).start()],
+        6: [lambda: finish_high(1, 1), lambda: finish_low(1)],
+        7: [lambda: finish_high(3, 3), lambda: finish_low(3), turn_corner],
+        8: [lambda: add_low(0)],
+    }
+    sequence = (6, 2, 5, 7, 4, 1, 3, 0)
+
+    def work(i, carry):
+        rest, previous = carry
+        d = lax.rem(rest, 8)
+
         @pl.when(i < 8)
         def _():
-            compute(i)
+            compute(d)
 
         @pl.when(i > 0)
         def _():
-            combine(i - 1)
-
-    for dy in range(1, 4):
-        high_along(4 + dy, dy).wait_recv()
-
-    @pl.loop(slab_rows // 2, slab_rows)
-    def _(z):
-        value = own[4, z]
-        for dy in range(1, 4):
-            value = value + from_y[4 + dy, z]
-        own[4, z] = value
-
-    high_across().start()
+            add_pair(previous)
+
+        for number, actions in plan.items():
+
+            @pl.when(i == number)
+            def _():
+                for action in actions:
+                    action()
+
+        return lax.div(rest, 8), d
+
+    lax.fori_loop(0, 9, work, (sum(d * 8**n for n, d in enumerate(sequence)), 0))
 
     loads[5].wait()
     stores = []
     for slot in range(measured.shape[0]):
 
-        @pl.loop(0, half)
+        @pl.loop(0, half, unroll=4)
         def _(row):
             both = jnp.concatenate([measured[slot, row], measured[slot, row + half]], 0)
             turned_over[slot, pl.ds(row, limit, half), :] = both.T
@@ -258,7 +298,7 @@
         )
 
     for part in range(2):
-        for dy in range(1, 4):
+        for dy in (1, 3):
             if part:
                 high_along(dy, dy).wait_recv()
             else:
@@ -268,9 +308,7 @@
 
         @pl.loop(part * slab_rows // 2, (part + 1) * slab_rows // 2)
         def _(z):
-            value = own[0, z]
-            for dy in range(1, 4):
-                value = value + from_y[dy, z]
+            value = own[0, z] + from_y[1, z] + from_y[3, z]
             if part:
                 value = value + from_x[0, z]
             total[:, z] = value
@@ -283,10 +321,13 @@
         to_pair(d).wait_send()
     for dy in range(4):
         low_across(dy).wait_send()
-        if dy:
-            low_along(dy).wait_send()
-            high_along(dy, dy).wait_send()
-            high_along(4 + dy, dy).wait_send()
+    for dy in (1, 3):
+        low_along(dy).wait_send()
+        high_along(dy, dy).wait_send()
+        high_along(4 + dy, dy).wait_send()
+        relay(2, 0, dy).wait_send()
+        relay(2, 1, dy).wait_send()
+        relay(6, 1, dy).wait_send()
     high_across().wait_send()
     for part in range(2):
         for d in range(1, 8):
@@ -329,7 +370,7 @@
         + [pltpu.VMEM((4,) + block[1:], I16)]
         + [pltpu.VMEM((slabs, slab_rows, share, tile), I16)]
         + [sem] * 5
-        + [pltpu.SemaphoreType.DMA((16,))] * 4,
+        + [pltpu.SemaphoreType.DMA((24,))] * 4,
         compiler_params=pltpu.CompilerParams(
             collective_id=1, has_side_effects=True, vmem_limit_bytes=56 * 2**20
         ),
@@ -528,7 +569,6 @@
 def collect_kernel(
     grads, pattern, out, mine, held, twin, counts, index, total, flat,
     slab_send, slab_recv, chip_send, chip_recv, pair_send, pair_recv,
-    low_send, low_recv, high_send, high_recv,
 ):
     slab, column = lax.axis_index("slab"), lax.axis_index("col")
     chip, core = lax.div(column, 2), lax.rem(column, 2)
@@ -540,7 +580,7 @@
     tiles = out.shape[1] // slab_rows
     columns = angles * tile_rows // (slabs * share)
     greet_near(slab, chip, core)
-    greeted(12)
+    greeted(11)
 
     order = [1, 3, 4, 2, 5, 7, 6]
     slabs_, chips, pairs = {}, {}, {}
@@ -565,23 +605,24 @@
 
     for d in order:
         slabs_[d].wait_recv()
-    low, high = slice(0, slab_rows // 2), slice(slab_rows // 2, slab_rows)
+    half, quarter = slab_rows // 2, slab_rows // 4
+    low, high = slice(0, half), slice(half, slab_rows)
+    upper, lower = slice(half, half + quarter), slice(half + quarter, slab_rows)
     across = (slab, 2 * moved(chip, (1, 0)) + core)
-    along = {dy: (slab, 2 * moved(chip, (0, dy)) + core) for dy in range(1, 4)}
-    for d in order[:4]:
-        chips[d] = remote(
-            mine, held.at[d], chip_send.at[d], chip_recv.at[d], across if d == 4 else along[d]
-        )
-        chips[d].start()
-    lows, highs = {}, {}
-    for dy in range(1, 4):
-        lows[dy] = remote(
-            held.at[dy, :, low], held.at[4 + dy, :, low], low_send.at[dy], low_recv.at[dy], across
-        )
-        highs[dy] = remote(
-            held.at[4, :, high], held.at[4 + dy, :, high], high_send.at[dy], high_recv.at[dy],
-            along[dy],
-        )
+    up = (slab, 2 * moved(chip, (0, 1)) + core)
+    down = (slab, 2 * moved(chip, (0, 3)) + core)
+
+    def pass_on(number, source, target, rows, device):
+        chips[number] = remote(
+            (mine if source == 0 else held.at[source]).at[:, rows], held.at[target, :, rows],
+            chip_send.at[number], chip_recv.at[number], device,
+        )
+        chips[number].start()
+
+    whole = slice(0, slab_rows)
+    pass_on(0, 0, 1, whole, up)
+    pass_on(1, 0, 3, whole, down)
+    pass_on(2, 0, 4, whole, across)
     pairs[0] = remote(mine, twin.at[0], pair_send.at[0], pair_recv.at[0], sibling)
     pairs[0].start()
 
@@ -631,24 +672,52 @@
                     result = result + total[span, lanes]
                 total[span, lanes] = result
 
-    pending = 0
-    for d in order + [None]:
-        if d is not None:
-            if d < 5:
-                chips[d].wait_recv()
-            else:
-                lows[d - 4].wait_recv()
-                highs[d - 4].wait_recv()
-            if d < 4:
-                lows[d].start()
-            elif d == 4:
-                for dy in range(1, 4):
-                    highs[dy].start()
-            pairs[d] = remote(held.at[d], twin.at[d], pair_send.at[d], pair_recv.at[d], sibling)
-            pairs[d].start()
-        pairs[pending].wait_recv()
-        add(pending, held.at[pending] if pending else mine, twin.at[pending])
-        pending = d
+    def arrived(*numbers):
+        for number in numbers:
+            chips[number].wait_recv()
+
+    def to_sibling(d):
+        pairs[d] = remote(held.at[d], twin.at[d], pair_send.at[d], pair_recv.at[d], sibling)
+        pairs[d].start()
+
+    def use(d):
+        pairs[d].wait_recv()
+        add(d, held.at[d] if d else mine, twin.at[d])
+
+    arrived(0)
+    pass_on(3, 1, 2, low, up)
+    pass_on(4, 1, 5, low, across)
+    to_sibling(1)
+    arrived(1)
+    pass_on(5, 3, 2, high, down)
+    pass_on(6, 3, 7, low, across)
+    to_sibling(3)
+    arrived(2)
+    pass_on(7, 4, 5, high, up)
+    pass_on(8, 4, 7, high, down)
+    to_sibling(4)
+    use(0)
+    arrived(3)
+    pass_on(9, 2, 6, low, across)
+    use(1)
+    arrived(7)
+    pass_on(10, 5, 6, upper, up)
+    arrived(8)
+    pass_on(11, 7, 6, lower, down)
+    use(3)
+    arrived(5)
+    to_sibling(2)
+    use(4)
+    arrived(4)
+    to_sibling(5)
+    use(2)
+    arrived(6)
+    to_sibling(7)
+    use(5)
+    arrived(9, 10, 11)
+    to_sibling(6)
+    use(7)
+    use(6)
 
     for k in range(group):
         for z in range(slab_rows):
@@ -658,11 +727,8 @@
 
     for d in order:
         slabs_[d].wait_send()
-    for d in order[:4]:
-        chips[d].wait_send()
-    for dy in range(1, 4):
-        lows[dy].wait_send()
-        highs[dy].wait_send()
+    for number in range(12):
+        chips[number].wait_send()
     for d in [0] + order:
         pairs[d].wait_send()
 
@@ -688,9 +754,9 @@
             pltpu.VMEM((group * tiles, slab_rows * tile), F32),
             pltpu.VMEM((tiles * slab_rows, tile), F32),
         ]
-        + [sem] * 10,
+        + [sem, sem, pltpu.SemaphoreType.DMA((12,)), pltpu.SemaphoreType.DMA((12,)), sem, sem],
         compiler_params=pltpu.CompilerParams(
-            collective_id=2, has_side_effects=True, vmem_limit_bytes=56 * 2**20
+            collective_id=2, has_side_effects=True, vmem_limit_bytes=32 * 2**20
         ),
     )(grads, pattern)
 
@@ -736,7 +802,7 @@
             block,
         ],
         out_specs=block,
-        compiler_params=pltpu.CompilerParams(vmem_limit_bytes=56 * 2**20),
+        compiler_params=pltpu.CompilerParams(vmem_limit_bytes=20 * 2**20),
     )(sums, templates, volume, consensus)
 
 

time: 107 us -> 96.1 us (0.90); the launches traced: 105 us -> 95.6 us
  Pallas kernels: 105 us -> 94.3 us
  local copies, waits for them, and re-layouts: 0 us -> 1.12 us
    pallas_call x1, Pallas kernels: 43.6 us -> 38.3 us  [collect(): pl.pallas_call(collect_kernel, out_shape=jax.ShapeDtypeStruct((group, til...]
    pallas_call x1, Pallas kernels: 41.8 us -> 38.7 us  [forward(): pl.pallas_call(forward_kernel, out_shape=(jax.ShapeDtypeStruct((slabs, sl...]
    pallas_call x1, Pallas kernels: 7.38 us -> 4.46 us  [update(): pl.pallas_call(update_kernel, grid=(steps,), out_shape=jax.ShapeDtypeStru...]
    unnamed x0 -> x10, local copies, waits for them, and re-layouts: none -> 1.12 us
where the time goes in v6:
time: 96.1 us; the launch traced here: 95.6 us
  Pallas kernels  94.3 us (98%)
  local copies, waits for them, and re-layouts  1.12 us (1%)
    pallas_call x1, Pallas kernels, forward(): pl.pallas_call(forward_kernel, out_shape=(jax.ShapeDtypeStruct((slabs, sl...  38.7 us
    pallas_call x1, Pallas kernels, collect(): pl.pallas_call(collect_kernel, out_shape=jax.ShapeDtypeStruct((group, til...  38.3 us
    pallas_call x1, Pallas kernels, ptycho(): pl.pallas_call(ptycho_kernel, out_shape=jax.ShapeDtypeStruct((height, til...  12.8 us
    pallas_call x1, Pallas kernels, update(): pl.pallas_call(update_kernel, grid=(steps,), out_shape=jax.ShapeDtypeStru...  4.46 us

profile of v6, /device:TPU:1, one launch (start us, length us, event | category | flops | bytes accessed | tf_op | source)
XLA Modules:
  0.0 95.6 jit_solution(4484463912027218985)
XLA Ops:
  0.0 38.7 %shard_map.118 = (s16[8,8,16,128]{3,2,1,0:T(8,128)(2,1)}, f32[2,4096,128]{2,1,0:T(8,128)}) custom-call(bf16[8,131072]{1,0:T(8,128)(2,1)} %volume.1, bf16[8,1024,128]{2,1,0:T(8,128)(2,1)} %templates.1, s32[8,8,256]{2,1,0:T(8,128)} %bitcast.7, f32[2,64,64,128]{3,2,1,0:T(8,128)} %bitcast.9), custom_call_target="tpu_custom_call" | custom-call | tf_op jit(solution)/shard_map/pallas_call | solution.py:351
  38.7 0.0 copy-start.4
  38.8 0.0 copy-start.1
  38.8 0.0 copy-start.2
  38.8 12.8 %shard_map.119 = bf16[1024,128]{1,0:T(8,128)(2,1)} custom-call(s32[256]{0:T(256)} %counts.1, s32[256,128]{1,0:T(8,128)} %starts_in.1, s16[1024,128]{1,0:T(8,128)(2,1)} %bitcast.10, f32[2,64,64]{2,1,0:T(8,128)} %probe_wave.1, bf16[256,256]{1,0:T(8,128)(2,1)} %constant.8.clone.t_first, bf16[256,256]{1,0:T(8,128)(2,1)} %constant.9.clone.t_pair, ...), custom_call_target="tpu_custom_call" | custom-call | tf_op jit(solution)/shard_map/pallas_call | solution.py:547
  51.6 0.0 copy-start
  51.6 0.0 copy-done.4
  51.6 0.0 copy-start.3
  51.7 1.1 %copy-done.3 = bf16[1024,128]{1,0:T(8,128)(2,1)S(1)} copy-done((bf16[1024,128]{1,0:T(8,128)(2,1)S(1)}, bf16[1024,128]{1,0:T(8,128)(2,1)}, u32[]{:S(2)}) %copy-start.3) | copy-done | bytes 262168
  52.7 38.3 %shard_map.120.sums = bf16[8,1024,128]{2,1,0:T(8,128)(2,1)S(1)} custom-call(bf16[8,8,16,128]{3,2,1,0:T(8,128)(2,1)S(1)} %bitcast.6, s32[8,8,256]{2,1,0:T(8,128)S(1)} %bitcast.8), custom_call_target="tpu_custom_call" | custom-call | tf_op jit(solution)/shard_map/pallas_call | solution.py:743
  91.1 0.0 copy-done.1
  91.1 0.0 copy-done.2
  91.1 0.0 copy-done
  91.1 4.5 %shard_map.121 = f32[8,131072]{1,0:T(8,128)} custom-call(bf16[8,1024,128]{2,1,0:T(8,128)(2,1)S(1)} %shard_map.120.sums, bf16[8,1024,128]{2,1,0:T(8,128)(2,1)S(1)} %copy-done.1, bf16[8,131072]{1,0:T(8,128)(2,1)S(1)} %copy-done, bf16[8,131072]{1,0:T(8,128)(2,1)S(1)} %copy-done.2), custom_call_target="tpu_custom_call" | custom-call | tf_op jit(solution)/shard_map/pallas_call | solution.py:794
Async XLA Ops:
  38.7 12.9 %copy-start.4 = (s32[1,256,8,8]{1,3,2,0:T(8,128)S(1)}, s32[1,256,8,8]{1,3,2,0:T(8,128)}, u32[]{:S(2)}) copy-start(s32[1,256,8,8]{1,3,2,0:T(8,128)} %param.15) | copy-start | bytes 196612
  38.8 52.3 %copy-start.1 = (bf16[8,1024,128]{2,1,0:T(8,128)(2,1)S(1)}, bf16[8,1024,128]{2,1,0:T(8,128)(2,1)}, u32[]{:S(2)}) copy-start(bf16[8,1024,128]{2,1,0:T(8,128)(2,1)} %templates.1) | copy-start | bytes 6291460
  38.8 52.3 %copy-start.2 = (bf16[8,131072]{1,0:T(8,128)(2,1)S(1)}, bf16[8,131072]{1,0:T(8,128)(2,1)}, u32[]{:S(2)}) copy-start(bf16[8,131072]{1,0:T(8,128)(2,1)} %consensus.1) | copy-start | bytes 6291460
  51.6 39.5 %copy-start = (bf16[8,131072]{1,0:T(8,128)(2,1)S(1)}, bf16[8,131072]{1,0:T(8,128)(2,1)}, u32[]{:S(2)}) copy-start(bf16[8,131072]{1,0:T(8,128)(2,1)} %volume.1) | copy-start | bytes 6291460
  51.6 1.1 %copy-start.3 = (bf16[1024,128]{1,0:T(8,128)(2,1)S(1)}, bf16[1024,128]{1,0:T(8,128)(2,1)}, u32[]{:S(2)}) copy-start(bf16[1024,128]{1,0:T(8,128)(2,1)} %shard_map.119) | copy-start | bytes 786436

commit v7 on v6

--- a/solution.py
+++ b/solution.py
@@ -11,7 +11,7 @@
 
 BF16 = jnp.bfloat16
 F32 = jnp.float32
-GROUP = 64
+GROUP = 128
 step_size = 0.1
 penalty = 1.0
 I16 = jnp.int16
@@ -433,7 +433,7 @@
 
 def ptycho_kernel(
     counts, starts_in, image, probe_wave, t_first, t_pair, t_pair_both, t_back, observed_in,
-    out, waves, total, staged, probe_a, probe_b, observed, starts, landed, here,
+    out, waves, swapped, total, staged, probe_a, probe_b, observed, starts, landed, here,
 ):
     slots = observed.shape[0]
     size = probe_wave.shape[1]
@@ -473,6 +473,7 @@
         for part in range(width // tile):
             sine, cosine = sine_cosine(staged[pl.ds(slot * (width // tile) + part, size, rows), :])
             waves[part * tile : (part + 1) * tile, :] = jnp.concatenate([cosine, sine], 0).T
+            swapped[part * tile : (part + 1) * tile, :] = jnp.concatenate([sine, cosine], 0).T
         total[...] = jnp.zeros_like(total)
         count = counts[first_angle + slot]
 
@@ -483,7 +484,7 @@
             exits = []
             for member in range(GROUP):
                 patch = waves[pl.ds(at[member], size), :]
-                exits.append(probe_a[...] * patch + probe_b[...] * pltpu.roll(patch, size, 1))
+                exits.append(probe_a[...] * patch + probe_b[...] * swapped[pl.ds(at[member], size), :])
             exit_wave = jnp.concatenate(exits, 0)
             high, low = halves(exit_wave)
             first = dot(jnp.concatenate([high, low], 1), t_first[...])
@@ -554,6 +555,7 @@
         scratch_shapes=[
             pltpu.VMEM((width, 2 * size), F32),
             pltpu.VMEM((width, 2 * size), F32),
+            pltpu.VMEM((width, 2 * size), F32),
             pltpu.VMEM((height, tile), F32),
             pltpu.VMEM((size, 2 * size), F32),
             pltpu.VMEM((size, 2 * size), F32),

time: 96.1 us -> 97.8 us (1.018)
  Pallas kernels: 94.3 us -> 96.4 us
    pallas_call x1, Pallas kernels: 12.8 us -> 19.6 us  [ptycho(): pl.pallas_call(ptycho_kernel, out_shape=jax.ShapeDtypeStruct((height, til...]
    pallas_call x1, Pallas kernels: 38.3 us -> 33.4 us  [collect(): pl.pallas_call(collect_kernel, out_shape=jax.ShapeDtypeStruct((group, til...]
where the time goes in v7:
time: 97.8 us; the launch traced here: 97.7 us
  Pallas kernels  96.4 us (99%)
  local copies, waits for them, and re-layouts  1.12 us (1%)
    pallas_call x1, Pallas kernels, forward(): pl.pallas_call(forward_kernel, out_shape=(jax.ShapeDtypeStruct((slabs, sl...  38.9 us
    pallas_call x1, Pallas kernels, collect(): pl.pallas_call(collect_kernel, out_shape=jax.ShapeDtypeStruct((group, til...  33.4 us
    pallas_call x1, Pallas kernels, ptycho(): pl.pallas_call(ptycho_kernel, out_shape=jax.ShapeDtypeStruct((height, til...  19.6 us
    pallas_call x1, Pallas kernels, update(): pl.pallas_call(update_kernel, grid=(steps,), out_shape=jax.ShapeDtypeStru...  4.46 us

profile of v7, /device:TPU:1, one launch (start us, length us, event | category | flops | bytes accessed | tf_op | source)
XLA Modules:
  0.0 97.7 jit_solution(8747513134694964895)
XLA Ops:
  0.0 38.9 %shard_map.118 = (s16[8,8,16,128]{3,2,1,0:T(8,128)(2,1)}, f32[2,4096,128]{2,1,0:T(8,128)}) custom-call(bf16[8,131072]{1,0:T(8,128)(2,1)} %volume.1, bf16[8,1024,128]{2,1,0:T(8,128)(2,1)} %templates.1, s32[8,8,256]{2,1,0:T(8,128)} %bitcast.7, f32[2,64,64,128]{3,2,1,0:T(8,128)} %bitcast.9), custom_call_target="tpu_custom_call" | custom-call | tf_op jit(solution)/shard_map/pallas_call | solution.py:351
  38.9 0.0 copy-start.4
  38.9 0.0 copy-start.1
  39.0 0.0 copy-start.2
  39.0 19.6 %shard_map.119 = bf16[1024,128]{1,0:T(8,128)(2,1)} custom-call(s32[256]{0:T(256)} %counts.1, s32[256,128]{1,0:T(8,128)} %starts_in.1, s16[1024,128]{1,0:T(8,128)(2,1)} %bitcast.10, f32[2,64,64]{2,1,0:T(8,128)} %probe_wave.1, bf16[256,256]{1,0:T(8,128)(2,1)} %constant.8.clone.t_first, bf16[256,256]{1,0:T(8,128)(2,1)} %constant.9.clone.t_pair, ...), custom_call_target="tpu_custom_call" | custom-call | tf_op jit(solution)/shard_map/pallas_call | solution.py:548
  58.6 0.0 copy-start
  58.6 0.0 copy-done.4
  58.6 0.0 copy-start.3
  58.6 1.1 %copy-done.3 = bf16[1024,128]{1,0:T(8,128)(2,1)S(1)} copy-done((bf16[1024,128]{1,0:T(8,128)(2,1)S(1)}, bf16[1024,128]{1,0:T(8,128)(2,1)}, u32[]{:S(2)}) %copy-start.3) | copy-done | bytes 262168
  59.7 33.4 %shard_map.120.sums = bf16[8,1024,128]{2,1,0:T(8,128)(2,1)S(1)} custom-call(bf16[8,8,16,128]{3,2,1,0:T(8,128)(2,1)S(1)} %bitcast.6, s32[8,8,256]{2,1,0:T(8,128)S(1)} %bitcast.8), custom_call_target="tpu_custom_call" | custom-call | tf_op jit(solution)/shard_map/pallas_call | solution.py:745
  93.2 0.0 copy-done.1
  93.2 0.0 copy-done.2
  93.2 0.0 copy-done
  93.2 4.5 %shard_map.121 = f32[8,131072]{1,0:T(8,128)} custom-call(bf16[8,1024,128]{2,1,0:T(8,128)(2,1)S(1)} %shard_map.120.sums, bf16[8,1024,128]{2,1,0:T(8,128)(2,1)S(1)} %copy-done.1, bf16[8,131072]{1,0:T(8,128)(2,1)S(1)} %copy-done, bf16[8,131072]{1,0:T(8,128)(2,1)S(1)} %copy-done.2), custom_call_target="tpu_custom_call" | custom-call | tf_op jit(solution)/shard_map/pallas_call | solution.py:796
Async XLA Ops:
  38.9 19.7 %copy-start.4 = (s32[1,256,8,8]{1,3,2,0:T(8,128)S(1)}, s32[1,256,8,8]{1,3,2,0:T(8,128)}, u32[]{:S(2)}) copy-start(s32[1,256,8,8]{1,3,2,0:T(8,128)} %param.15) | copy-start | bytes 196612
  38.9 54.2 %copy-start.1 = (bf16[8,1024,128]{2,1,0:T(8,128)(2,1)S(1)}, bf16[8,1024,128]{2,1,0:T(8,128)(2,1)}, u32[]{:S(2)}) copy-start(bf16[8,1024,128]{2,1,0:T(8,128)(2,1)} %templates.1) | copy-start | bytes 6291460
  39.0 54.2 %copy-start.2 = (bf16[8,131072]{1,0:T(8,128)(2,1)S(1)}, bf16[8,131072]{1,0:T(8,128)(2,1)}, u32[]{:S(2)}) copy-start(bf16[8,131072]{1,0:T(8,128)(2,1)} %consensus.1) | copy-start | bytes 6291460
  58.6 34.6 %copy-start = (bf16[8,131072]{1,0:T(8,128)(2,1)S(1)}, bf16[8,131072]{1,0:T(8,128)(2,1)}, u32[]{:S(2)}) copy-start(bf16[8,131072]{1,0:T(8,128)(2,1)} %volume.1) | copy-start | bytes 6291460
  58.6 1.1 %copy-start.3 = (bf16[1024,128]{1,0:T(8,128)(2,1)S(1)}, bf16[1024,128]{1,0:T(8,128)(2,1)}, u32[]{:S(2)}) copy-start(bf16[1024,128]{1,0:T(8,128)(2,1)} %shard_map.119) | copy-start | bytes 786436

commit v8 on v7

--- a/solution.py
+++ b/solution.py
@@ -11,7 +11,7 @@
 
 BF16 = jnp.bfloat16
 F32 = jnp.float32
-GROUP = 128
+GROUP = 64
 step_size = 0.1
 penalty = 1.0
 I16 = jnp.int16
@@ -791,7 +791,7 @@
 def update(sums, templates, volume, consensus):
     slab_rows, cells = volume.shape
     group, height, tile = sums.shape
-    steps = 4
+    steps = 2
     block = pl.BlockSpec((slab_rows, cells // steps), lambda i: (0, i))
     return pl.pallas_call(
         update_kernel,

time: 97.8 us -> 96.5 us (0.987); the launches traced: 97.7 us -> 97.4 us
    pallas_call x1, Pallas kernels: 33.4 us -> 40.5 us  [collect(): pl.pallas_call(collect_kernel, out_shape=jax.ShapeDtypeStruct((group, til...]
    pallas_call x1, Pallas kernels: 19.6 us -> 12.6 us  [ptycho(): pl.pallas_call(ptycho_kernel, out_shape=jax.ShapeDtypeStruct((height, til...]
where the time goes in v8:
time: 96.5 us; the launch traced here: 97.4 us
  Pallas kernels  96.1 us (100%)
  local copies, waits for them, and re-layouts  1.12 us (1%)
    pallas_call x1, Pallas kernels, collect(): pl.pallas_call(collect_kernel, out_shape=jax.ShapeDtypeStruct((group, til...  40.5 us
    pallas_call x1, Pallas kernels, forward(): pl.pallas_call(forward_kernel, out_shape=(jax.ShapeDtypeStruct((slabs, sl...  38.7 us
    pallas_call x1, Pallas kernels, ptycho(): pl.pallas_call(ptycho_kernel, out_shape=jax.ShapeDtypeStruct((height, til...  12.6 us
    pallas_call x1, Pallas kernels, update(): pl.pallas_call(update_kernel, grid=(steps,), out_shape=jax.ShapeDtypeStru...  4.24 us

profile of v8, /device:TPU:1, one launch (start us, length us, event | category | flops | bytes accessed | tf_op | source)
XLA Modules:
  0.0 97.4 jit_solution(17534188583187083926)
XLA Ops:
  0.0 38.7 %shard_map.118 = (s16[8,8,16,128]{3,2,1,0:T(8,128)(2,1)}, f32[2,4096,128]{2,1,0:T(8,128)}) custom-call(bf16[8,131072]{1,0:T(8,128)(2,1)} %volume.1, bf16[8,1024,128]{2,1,0:T(8,128)(2,1)} %templates.1, s32[8,8,256]{2,1,0:T(8,128)} %bitcast.7, f32[2,64,64,128]{3,2,1,0:T(8,128)} %bitcast.9), custom_call_target="tpu_custom_call" | custom-call | tf_op jit(solution)/shard_map/pallas_call | solution.py:351
  38.7 0.0 copy-start.4
  38.8 0.0 copy-start.1
  38.8 0.0 copy-start.2
  38.8 12.6 %shard_map.119 = bf16[1024,128]{1,0:T(8,128)(2,1)} custom-call(s32[256]{0:T(256)} %counts.1, s32[256,128]{1,0:T(8,128)} %starts_in.1, s16[1024,128]{1,0:T(8,128)(2,1)} %bitcast.10, f32[2,64,64]{2,1,0:T(8,128)} %probe_wave.1, bf16[256,256]{1,0:T(8,128)(2,1)} %constant.8.clone.t_first, bf16[256,256]{1,0:T(8,128)(2,1)} %constant.9.clone.t_pair, ...), custom_call_target="tpu_custom_call" | custom-call | tf_op jit(solution)/shard_map/pallas_call | solution.py:548
  51.4 0.0 copy-start
  51.4 0.0 copy-done.4
  51.4 0.0 copy-start.3
  51.4 1.1 %copy-done.3 = bf16[1024,128]{1,0:T(8,128)(2,1)S(1)} copy-done((bf16[1024,128]{1,0:T(8,128)(2,1)S(1)}, bf16[1024,128]{1,0:T(8,128)(2,1)}, u32[]{:S(2)}) %copy-start.3) | copy-done | bytes 262168
  52.5 40.5 %shard_map.120.sums = bf16[8,1024,128]{2,1,0:T(8,128)(2,1)S(1)} custom-call(bf16[8,8,16,128]{3,2,1,0:T(8,128)(2,1)S(1)} %bitcast.6, s32[8,8,256]{2,1,0:T(8,128)S(1)} %bitcast.8), custom_call_target="tpu_custom_call" | custom-call | tf_op jit(solution)/shard_map/pallas_call | solution.py:745
  93.1 0.0 copy-done.1
  93.1 0.0 copy-done.2
  93.1 0.0 copy-done
  93.1 4.2 %shard_map.121 = f32[8,131072]{1,0:T(8,128)} custom-call(bf16[8,1024,128]{2,1,0:T(8,128)(2,1)S(1)} %shard_map.120.sums, bf16[8,1024,128]{2,1,0:T(8,128)(2,1)S(1)} %copy-done.1, bf16[8,131072]{1,0:T(8,128)(2,1)S(1)} %copy-done, bf16[8,131072]{1,0:T(8,128)(2,1)S(1)} %copy-done.2), custom_call_target="tpu_custom_call" | custom-call | tf_op jit(solution)/shard_map/pallas_call | solution.py:796
Async XLA Ops:
  38.7 12.7 %copy-start.4 = (s32[1,256,8,8]{1,3,2,0:T(8,128)S(1)}, s32[1,256,8,8]{1,3,2,0:T(8,128)}, u32[]{:S(2)}) copy-start(s32[1,256,8,8]{1,3,2,0:T(8,128)} %param.15) | copy-start | bytes 196612
  38.8 54.3 %copy-start.1 = (bf16[8,1024,128]{2,1,0:T(8,128)(2,1)S(1)}, bf16[8,1024,128]{2,1,0:T(8,128)(2,1)}, u32[]{:S(2)}) copy-start(bf16[8,1024,128]{2,1,0:T(8,128)(2,1)} %templates.1) | copy-start | bytes 6291460
  38.8 54.3 %copy-start.2 = (bf16[8,131072]{1,0:T(8,128)(2,1)S(1)}, bf16[8,131072]{1,0:T(8,128)(2,1)}, u32[]{:S(2)}) copy-start(bf16[8,131072]{1,0:T(8,128)(2,1)} %consensus.1) | copy-start | bytes 6291460
  51.4 41.7 %copy-start = (bf16[8,131072]{1,0:T(8,128)(2,1)S(1)}, bf16[8,131072]{1,0:T(8,128)(2,1)}, u32[]{:S(2)}) copy-start(bf16[8,131072]{1,0:T(8,128)(2,1)} %volume.1) | copy-start | bytes 6291460
  51.4 1.1 %copy-start.3 = (bf16[1024,128]{1,0:T(8,128)(2,1)S(1)}, bf16[1024,128]{1,0:T(8,128)(2,1)}, u32[]{:S(2)}) copy-start(bf16[1024,128]{1,0:T(8,128)(2,1)} %shard_map.119) | copy-start | bytes 786436
